TPU v7x, 32 devices: a whole 2x2x4 slice. The times are simulated.
32 devices in a mesh: tracer: 4 (over y, x), domain: 8 (over z, core).
Axes of the slice: x: 2, y: 2, z: 4, core: 2. Of those that a mesh axis runs over, the one named last changes fastest.
Arguments:
- log_rate: float32 [128, 256, 256], P('domain'), may hold values from -1.6 to 0
- velocity: float32 [256, 256], replicated, may hold values from 0.2 to 1
- initial: float32 [4, 128, 256, 256], P('tracer', 'domain'), may hold values from -6 to 6
- profile: float32 [4, 256, 256], P('tracer'), may hold values from 0.5 to 4
- plane: int32 [4], P('tracer'), may hold values from 0 to 127
- depth: int32 [4, 32768], P('tracer'), may hold values from 0 to 127
- row: int32 [4, 32768], P('tracer'), may hold values from 0 to 255
- column: int32 [4, 32768], P('tracer'), may hold values from 0 to 255
- step_of: int32 [4, 32768], P('tracer'), may hold values from 1 to 2
- observed: float32 [4, 32768], P('tracer'), may hold values from -6 to 6
Outputs:
- smoothed_gradient: float32 [64, 128, 128], P('domain', 'tracer')
All inputs are finite; a program needn't handle non-finite values.
Results may differ from a plain program's by a relative error of at most 0.0003.
Values sent between devices are 32-bit elements; how exact they have to be, the bound alone decides.
A program may use at most 512 MiB of HBM per device.

v0:
```python
import math

import jax
import jax.numpy as jnp
from jax import lax
from jax.sharding import PartitionSpec as P

R = 2
STEPS = 2


TIME_STEP = 0.14
PRIOR_RANGE = 4.0


def extended(array, sides, width):
    for axis, dim in sides:
        count, length = (lax.axis_size(axis), array.shape[dim])
        up = [(i, (i + 1) % count) for i in range(count)]
        down = [(j, i) for i, j in up]
        last = lax.slice_in_dim(array, length - width, length, axis=dim)
        initial = lax.slice_in_dim(array, 0, width, axis=dim)
        before = lax.ppermute(last, axis, up)
        after = lax.ppermute(initial, axis, down)
        array = jnp.concatenate([before, array, after], axis=dim)
    return array


def diffusion(padded, faces):
    values = padded[1:-1]
    result = faces[0] * (padded[2:] - values) - faces[1] * (values - padded[:-2])
    for axis_dim, face_now, face_back in ((1, faces[2], faces[3]), (2, faces[4], faces[5])):
        ahead_cell = jnp.roll(values, -1, axis_dim)
        behind_cell = jnp.roll(values, 1, axis_dim)
        result = result + face_now * (ahead_cell - values) - face_back * (values - behind_cell)
    return result


def sensitivity(state_pad, adjoint_pad):
    state = state_pad[1:-1]
    adjoint = adjoint_pad[1:-1]
    upper_term = (state_pad[2:] - state) * (adjoint_pad[2:] - adjoint)
    lower_term = (state - state_pad[:-2]) * (adjoint - adjoint_pad[:-2])
    result = upper_term + lower_term
    for axis_dim in (1, 2):
        product = (jnp.roll(state, -1, axis_dim) - state) * (
            jnp.roll(adjoint, -1, axis_dim) - adjoint
        )
        result = result + product + jnp.roll(product, 1, axis_dim)
    return -0.5 * result


def hartley(length, first_row, count):
    indices = first_row + lax.iota(jnp.int32, count)
    phases = indices[:, None] * lax.iota(jnp.int32, length)[None, :] % length
    angles = 2.0 * math.pi / length * phases.astype(jnp.float32)
    return jnp.cos(angles) + jnp.sin(angles)


def transform(table, values, axis_dim):
    forms = ("kj,jab->kab", "kj,ajb->akb", "kj,abj->abk")
    return jnp.einsum(
        forms[axis_dim],
        table,
        values,
        precision=lax.Precision.HIGHEST,
        preferred_element_type=jnp.float32,
    )


def symbol_part(length, first_row, count):
    indices = (first_row + lax.iota(jnp.int32, count)) % length
    angles = 2.0 * math.pi / length * indices.astype(jnp.float32)
    return 2.0 - 2.0 * jnp.cos(angles)


def prior_weights(
    depth_span,
    depth_first,
    depth_count,
    first_span,
    first_start,
    first_count,
    second_span,
    second_start,
    second_count,
):
    lam_sum = (
        symbol_part(depth_span, depth_first, depth_count)[:, None, None]
        + symbol_part(first_span, first_start, first_count)[None, :, None]
        + symbol_part(second_span, second_start, second_count)[None, None, :]
    )
    factor = 1.0 + PRIOR_RANGE * lam_sum
    return 1.0 / (factor * factor) / (depth_span * first_span * second_span)


def local(log_rate, velocity, initial, profile, plane, depth, row, column, step_of, observed):
    slab_depth, rows_count, cols_count = log_rate.shape
    offset = lax.axis_index("domain") * slab_depth
    kappa_field = jnp.exp(log_rate)
    kappa_pad = extended(kappa_field, (("domain", 0),), 1)
    face_first = 0.5 * (kappa_field + jnp.roll(kappa_field, -1, 1))
    face_second = 0.5 * (kappa_field + jnp.roll(kappa_field, -1, 2))
    faces = (
        0.5 * (kappa_pad[1:-1] + kappa_pad[2:]),
        0.5 * (kappa_pad[:-2] + kappa_pad[1:-1]),
        face_first,
        jnp.roll(face_first, 1, 1),
        face_second,
        jnp.roll(face_second, 1, 2),
    )
    layers = offset + lax.iota(jnp.int32, slab_depth)
    source = jnp.where((layers == plane[0])[:, None, None], profile[0][None], 0.0)
    wind = velocity[None]
    local_depth = depth[0] - offset
    inside = (local_depth >= 0) & (local_depth < slab_depth)
    flat = (
        jnp.clip(local_depth, 0, slab_depth - 1) * (rows_count * cols_count)
        + row[0] * cols_count
        + column[0]
    )
    probe_steps = step_of[0]
    states = []
    values = initial[0]
    sampled = jnp.zeros_like(observed[0])
    for section in range(STEPS):
        padded = extended(values, (("domain", 0),), 1)
        states.append(padded)
        values = (
            padded[1:-1]
            + TIME_STEP * (diffusion(padded, faces) - wind * (padded[1:-1] - padded[:-2]))
            + TIME_STEP * source
        )
        sampled = jnp.where(probe_steps == section + 1, values.reshape(-1)[flat], sampled)
    residual = jnp.where(inside, sampled - observed[0], 0.0)

    def inject(section):
        empty = jnp.zeros((slab_depth * rows_count * cols_count,), log_rate.dtype)
        return (
            empty.at[flat]
            .add(jnp.where(probe_steps == section, residual, 0.0))
            .reshape(log_rate.shape)
        )

    adjoint = inject(STEPS)
    gradient = jnp.zeros_like(log_rate)
    for section in reversed(range(STEPS)):
        adjoint_pad = extended(adjoint, (("domain", 0),), 1)
        gradient = gradient + sensitivity(states[section], adjoint_pad)
        if section > 0:
            adjoint = (
                adjoint_pad[1:-1]
                + TIME_STEP
                * (diffusion(adjoint_pad, faces) - wind * (adjoint_pad[1:-1] - adjoint_pad[2:]))
                + inject(section)
            )
    fine_grad = TIME_STEP * kappa_field * gradient
    coarse = fine_grad.reshape(slab_depth // R, R, rows_count // R, R, cols_count // R, R).sum(
        axis=(1, 3, 5)
    )
    coarse_depth, first_size, second_size = coarse.shape
    domain_count = lax.axis_size("domain")
    tracer_count = lax.axis_size("tracer")
    share_rows = first_size // tracer_count
    own_first = lax.axis_index("tracer") * share_rows
    summed = lax.psum(coarse, "tracer")
    spectral = transform(hartley(first_size, 0, first_size), summed, 1)
    spectral = transform(hartley(second_size, 0, second_size), spectral, 2)
    columns = lax.all_to_all(spectral, "domain", split_axis=1, concat_axis=0, tiled=True)
    full_depth = columns.shape[0]
    block_width = first_size // domain_count
    depth_table = hartley(full_depth, 0, full_depth)
    columns = transform(depth_table, columns, 0)
    columns = columns * prior_weights(
        full_depth,
        0,
        full_depth,
        first_size,
        lax.axis_index("domain") * block_width,
        block_width,
        second_size,
        0,
        second_size,
    )
    columns = transform(depth_table, columns, 0)
    returned = lax.all_to_all(columns, "domain", split_axis=0, concat_axis=1, tiled=True)
    returned = transform(hartley(second_size, 0, second_size), returned, 2)
    result = transform(hartley(first_size, own_first, share_rows), returned, 1)
    return result


def solution(mesh):
    return jax.shard_map(
        local,
        mesh=mesh,
        in_specs=(
            P("domain", None, None),
            P(),
            P("tracer", "domain", None, None),
            P("tracer", None, None),
            P("tracer"),
            P("tracer", None),
            P("tracer", None),
            P("tracer", None),
            P("tracer", None),
            P("tracer", None),
        ),
        out_specs=P("domain", "tracer", None),
        check_vma=False,
    )
```

profile of v0, /device:TPU:0, one launch (start us, length us, event | category | flops | bytes accessed | tf_op | source)
XLA Modules:
  0.0 1817.5 jit_solution(7049587821993194920)
XLA Ops:
  10.4 4.5 collective-permute-start
  25.0 4.7 fusion.154
  40.2 5.7 fusion.28
  46.5 4.4 copy-done.4
  51.6 16.6 fusion.36
  68.3 4.8 fusion.149
  88.8 387.3 %gather_fusion.1 = f32[32768]{0:T(1024)S(1)} fusion(f32[1048576]{0:T(1024)} %bitcast.57, s32[32768]{0:T(1024)S(1)} %copy-done.16), kind=kCustom, calls=%fused_computation.1 | custom fusion | bytes 393216 | tf_op jit(solution)/shard_map/gather | solution.py:134
  477.1 22.5 %fusion.46 = f32[16,256,256]{2,1,0:T(8,128)S(1)} fusion(f32[16,256,256]{2,1,0:T(8,128)} %copy-done, f32[16,255,256]{2,1,0:T(8,128)} %get-tuple-element.30, f32[16,1,256]{2,1,0:T(1,128)S(1)} %get-tuple-element.32, f32[16,256,255]{2,1,0:T(8,128)} %get-tuple-element.26, f32[16,256,1]{2,1,0:T(8,128)} %get-tuple-element.28, f32[16,256,256]{2,1,0:T(8,128)} %copy-done.6, ...), kind=kLoop, calls=%fused_computation.70 | loop fusion | flops 39845888 | bytes 47710224 | tf_op jit(solution)/shard_map/add | solution.py:130
  503.9 387.3 %gather_fusion = f32[32768]{0:T(1024)S(1)} fusion(f32[1048576]{0:T(1024)} %bitcast.56, s32[32768]{0:T(1024)S(1)} %copy-done.16), kind=kCustom, calls=%fused_computation | custom fusion | bytes 393216 | tf_op jit(solution)/shard_map/gather | solution.py:134
  891.3 173.9 %scatter_custom_fusion = f32[1048576]{0:T(1024)} fusion(s32[32768]{0:T(1024)} %bitcast.82, f32[32768]{0:T(1024)S(1)} %get-tuple-element.7, f32[]{:T(128)} %constant.108.clone.1), kind=kCustom, calls=%fused_computation.93 | custom fusion | flops 32768 | bytes 4194816 | tf_op jit(solution)/shard_map/scatter-add | solution.py:141
  1065.2 5.3 reshape.196
  1070.5 8.2 fusion.144
  1092.0 10.8 fusion.61
  1107.4 173.3 %scatter_custom_fusion.1 = f32[1048576]{0:T(1024)} fusion(s32[32768]{0:T(1024)} %bitcast.83, f32[32768]{0:T(1024)} %broadcast_select_fusion.1, f32[]{:T(128)} %constant.108.clone.1), kind=kCustom, calls=%fused_computation.91 | custom fusion | flops 32768 | bytes 4194816 | tf_op jit(solution)/shard_map/scatter-add | solution.py:141
  1280.8 5.2 reshape.197
  1286.0 23.6 %fusion.19 = f32[16,256,256]{2,1,0:T(8,128)S(1)} fusion(f32[16,256,256]{2,1,0:T(8,128)} %reshape.197, f32[16,256,256]{2,1,0:T(8,128)} %reshape.196, f32[1,256,256]{2,1,0:T(8,128)S(1)} %collective-permute-done.6, f32[16,255,256]{2,1,0:T(8,128)} %get-tuple-element.20, f32[16,1,256]{2,1,0:T(1,128)S(1)} %get-tuple-element.22, ...), kind=kLoop, calls=%fused_computation.27 | loop fusion | flops 38797312 | bytes 51642368 | tf_op jit(solution)/shard_map/add | solution.py:152
  1322.4 8.3 fusion.55
  1335.8 29.1 %fusion.9 = f32[16,256,256]{2,1,0:T(8,128)} fusion(f32[16,256,256]{2,1,0:T(8,128)} %copy-done.11, f32[16,256,256]{2,1,0:T(8,128)} %get-tuple-element.11, f32[16,256,256]{2,1,0:T(8,128)} %copy-done.9, f32[1,256,256]{2,1,0:T(8,128)} %collective-permute-done.9, f32[1,256,256]{2,1,0:T(8,128)} %collective-permute-done.8, f32[16,256,256]{2,1,0:T(8,128)} %copy-done.10, ...), kind=kLoop, calls=%fused_computation.14 | loop fusion | flops 39845888 | bytes 60817408 | tf_op jit(solution)/shard_map/mul | solution.py:157
  1364.8 270.4 %reshape.198 = f32[8,2,128,2,128,2]{5,4,3,2,1,0:T(8,128)} reshape(f32[16,256,256]{2,1,0:T(8,128)} %fusion.9) | data formatting | bytes 8388608 | tf_op jit(solution)/shard_map/reshape | solution.py:158
  1635.2 80.2 %reduce_sum.9 = f32[8,128,128]{2,1,0:T(8,128)S(1)} reduce(f32[8,2,128,2,128,2]{5,4,3,2,1,0:T(8,128)} %reshape.198, f32[]{:T(128)} %constant.108.clone.1), dimensions={1,3,5}, to_apply=%region_2.3 | reduce | flops 917504 | bytes 4718596 | tf_op jit(solution)/shard_map/reduce_sum | solution.py:158
  1716.5 46.6 %all-reduce.2.cloned.1.call-done = f32[8,128,128]{1,2,0:T(8,128)} async-done(((f32[8,128,128]{1,2,0:T(8,128)}), f32[8,128,128]{1,2,0:T(8,128)}) %all-reduce.2.cloned.1.call-update) | async-done | bytes 524304 | tf_op jit(solution)/shard_map/psum | solution.py:166
  1766.9 4.6 all-to-all-start
  1771.7 15.1 all-to-all-done
  1793.1 15.3 all-to-all-done.1
  (145 shorter events, 95.0 us)
Async XLA Ops:
  6.5 1756.6 %all-reduce.2.cloned.1.call-start = ((), (), s32[]{:S(2)}) async-start(), calls=%async_computation.2 | async-start | bytes 1048576 | tf_op jit(solution)/shard_map/psum | solution.py:166
  10.4 41.2 %collective-permute-start = (f32[1,256,256]{2,1,0:T(8,128)}, f32[1,256,256]{2,1,0:T(8,128)S(1)}, u32[]{:S(2)}, u32[]{:S(2)}) collective-permute-start(f32[1,256,256]{2,1,0:T(8,128)} %get-tuple-element.44), channel_id=1, source_target_pairs={{1,0},{2,1},{3,2},{4,3},{5,4},{6,5},{7,6},{0,7},{9,8},{10,9},{11,1... | collective-permute-start | bytes 786440 | tf_op jit(solution)/shard_map/ppermute | solution.py:24
  14.9 36.7 %collective-permute-start.2 = (f32[1,256,256]{2,1,0:T(8,128)}, f32[1,256,256]{2,1,0:T(8,128)}, u32[]{:S(2)}, u32[]{:S(2)}) collective-permute-start(f32[1,256,256]{2,1,0:T(8,128)} %get-tuple-element.43), channel_id=1, source_target_pairs={{0,1},{1,2},{2,3},{3,4},{4,5},{5,6},{6,7},{7,0},{8,9},{9,10},{10,1... | collective-permute-start | bytes 786440 | tf_op jit(solution)/shard_map/ppermute | solution.py:23
  15.8 35.8 %collective-permute-start.1 = (f32[1,256,256]{2,1,0:T(8,128)}, f32[1,256,256]{2,1,0:T(8,128)}, u32[]{:S(2)}, u32[]{:S(2)}) collective-permute-start(f32[1,256,256]{2,1,0:T(8,128)} %get-tuple-element.45), channel_id=1, source_target_pairs={{1,0},{2,1},{3,2},{4,3},{5,4},{6,5},{7,6},{0,7},{9,8},{10,9},{11,1... | collective-permute-start | bytes 786440 | tf_op jit(solution)/shard_map/ppermute | solution.py:24
  19.3 32.3 %collective-permute-start.3 = (f32[1,256,256]{2,1,0:T(8,128)}, f32[1,256,256]{2,1,0:T(8,128)}, u32[]{:S(2)}, u32[]{:S(2)}) collective-permute-start(f32[1,256,256]{2,1,0:T(8,128)} %get-tuple-element.46), channel_id=1, source_target_pairs={{0,1},{1,2},{2,3},{3,4},{4,5},{5,6},{6,7},{7,0},{8,9},{9,10},{10,1... | collective-permute-start | bytes 786440 | tf_op jit(solution)/shard_map/ppermute | solution.py:23
  45.8 22.4 %copy-start.6 = (f32[16,256,256]{2,1,0:T(8,128)}, f32[16,256,256]{2,1,0:T(8,128)S(1)}, u32[]{:S(2)}) copy-start(f32[16,256,256]{2,1,0:T(8,128)S(1)} %get-tuple-element.48) | copy-start | bytes 12582916
  45.8 22.4 %copy-start.7 = (f32[16,256,256]{2,1,0:T(8,128)}, f32[16,256,256]{2,1,0:T(8,128)S(1)}, u32[]{:S(2)}) copy-start(f32[16,256,256]{2,1,0:T(8,128)S(1)} %get-tuple-element.47) | copy-start | bytes 12582916
  68.3 16.3 copy-start
  78.1 399.0 %collective-permute-start.4 = (f32[1,256,256]{2,1,0:T(8,128)}, f32[1,256,256]{2,1,0:T(8,128)S(1)}, u32[]{:S(2)}, u32[]{:S(2)}) collective-permute-start(f32[1,256,256]{2,1,0:T(8,128)} %get-tuple-element.33), channel_id=1, source_target_pairs={{1,0},{2,1},{3,2},{4,3},{5,4},{6,5},{7,6},{0,7},{9,8},{10,9},{11,1... | collective-permute-start | bytes 786440 | tf_op jit(solution)/shard_map/ppermute | solution.py:24
  81.7 395.5 %collective-permute-start.5 = (f32[1,256,256]{2,1,0:T(8,128)}, f32[1,256,256]{2,1,0:T(8,128)}, u32[]{:S(2)}, u32[]{:S(2)}) collective-permute-start(f32[1,256,256]{2,1,0:T(8,128)} %get-tuple-element.34), channel_id=1, source_target_pairs={{0,1},{1,2},{2,3},{3,4},{4,5},{5,6},{6,7},{7,0},{8,9},{9,10},{10,1... | collective-permute-start | bytes 786440 | tf_op jit(solution)/shard_map/ppermute | solution.py:23
  88.8 388.4 %copy-start.17 = (f32[1,256,256]{2,1,0:T(8,128)S(1)}, f32[1,256,256]{2,1,0:T(8,128)}, u32[]{:S(2)}) copy-start(f32[1,256,256]{2,1,0:T(8,128)} %param.13) | copy-start | bytes 786436
  477.1 22.5 %copy-start.18 = (f32[1,256,256]{2,1,0:T(8,128)}, f32[1,256,256]{2,1,0:T(8,128)S(1)}, u32[]{:S(2)}) copy-start(f32[1,256,256]{2,1,0:T(8,128)S(1)} %collective-permute-done.4) | copy-start | bytes 786436
  503.9 387.3 %copy-start.25 = (pred[32768]{0:T(1024)(128)(4,1)S(1)}, pred[32768]{0:T(1024)(128)(4,1)}, u32[]{:S(2)}) copy-start(pred[32768]{0:T(1024)(128)(4,1)} %get-tuple-element.6) | copy-start | bytes 98308
  503.9 387.3 %copy-start.30 = (f32[1,32768]{1,0:T(1,128)S(1)}, f32[1,32768]{1,0:T(1,128)}, u32[]{:S(2)}) copy-start(f32[1,32768]{1,0:T(1,128)} %param.19) | copy-start | bytes 393220
  503.9 387.3 %copy-start.31 = (pred[32768]{0:T(1024)(128)(4,1)S(1)}, pred[32768]{0:T(1024)(128)(4,1)}, u32[]{:S(2)}) copy-start(pred[32768]{0:T(1024)(128)(4,1)} %get-tuple-element.5) | copy-start | bytes 98308
  503.9 387.3 %copy-start.32 = (pred[32768]{0:T(1024)(128)(4,1)S(1)}, pred[32768]{0:T(1024)(128)(4,1)}, u32[]{:S(2)}) copy-start(pred[32768]{0:T(1024)(128)(4,1)} %get-tuple-element.49) | copy-start | bytes 98308
  1087.3 198.7 %collective-permute-start.6 = (f32[1,256,256]{2,1,0:T(8,128)S(1)}, f32[1,256,256]{2,1,0:T(8,128)S(1)}, u32[]{:S(2)}, u32[]{:S(2)}) collective-permute-start(f32[1,256,256]{2,1,0:T(8,128)S(1)} %slice.298), channel_id=1, source_target_pairs={{1,0},{2,1},{3,2},{4,3},{5,4},{6,5},{7,6},{0,7},{9,8},{10,9},{11,1... | collective-permute-start | bytes 786440 | tf_op jit(solution)/shard_map/ppermute | solution.py:24
  1092.0 194.0 %collective-permute-start.7 = (f32[1,256,256]{2,1,0:T(8,128)}, f32[1,256,256]{2,1,0:T(8,128)S(1)}, u32[]{:S(2)}, u32[]{:S(2)}) collective-permute-start(f32[1,256,256]{2,1,0:T(8,128)} %slice.301), channel_id=1, source_target_pairs={{0,1},{1,2},{2,3},{3,4},{4,5},{5,6},{6,7},{7,0},{8,9},{9,10},{10,1... | collective-permute-start | bytes 786440 | tf_op jit(solution)/shard_map/ppermute | solution.py:23
  1286.0 23.6 %copy-start.20 = (f32[1,256,256]{2,1,0:T(8,128)}, f32[1,256,256]{2,1,0:T(8,128)S(1)}, u32[]{:S(2)}) copy-start(f32[1,256,256]{2,1,0:T(8,128)S(1)} %collective-permute-done.6) | copy-start | bytes 786436
  1286.0 23.6 %copy-start.22 = (f32[1,256,256]{2,1,0:T(8,128)}, f32[1,256,256]{2,1,0:T(8,128)S(1)}, u32[]{:S(2)}) copy-start(f32[1,256,256]{2,1,0:T(8,128)S(1)} %collective-permute-done.7) | copy-start | bytes 786436
  1318.7 17.1 collective-permute-start.8
  1322.2 13.5 collective-permute-start.9
  1766.9 20.0 %all-to-all-start = ((f32[8,128,128]{2,0,1:T(8,128)}), f32[8,128,128]{2,0,1:T(8,128)S(1)}, u32[]{:S(2)}, u32[]{:S(2)}) async-start(f32[8,128,128]{2,0,1:T(8,128)} %fusion.68), calls=%async_computation | async-start | bytes 1048576 | tf_op jit(solution)/shard_map/all_to_all | solution.py:169
  1789.6 18.8 %all-to-all-start.1 = ((f32[64,16,128]{2,1,0:T(8,128)}), f32[64,16,128]{2,1,0:T(8,128)S(1)}, u32[]{:S(2)}, u32[]{:S(2)}) async-start(f32[64,16,128]{2,1,0:T(8,128)} %copy.30), calls=%async_computation.1 | async-start | bytes 1048576 | tf_op jit(solution)/shard_map/all_to_all | solution.py:186
  (24 other events, 165.5 us)
Sparse Core Ops, SparseCore 0:
  1716.6 46.4 all-reduce.1
where the time goes:
time: 1850 us; the launch traced here: 1820 us
  local copies, waits for them, and re-layouts  1140 us (62%)
  other arithmetic  548 us (30%)
  waiting for transfers between devices  77.1 us (4%)
  starting transfers between devices  27.5 us (1%)
    gather x2, local copies, waits for them, and re-layouts, local(): values.reshape(-1)[flat]  775 us
    scatter-add x2, other arithmetic, inject(): return empty.at[flat].add(jnp.where(probe_steps == section, residual, 0.0...  347 us
    reshape x1, local copies, waits for them, and re-layouts, local(): fine_grad.reshape(slab_depth // R, R, rows_count // R, R, cols_count // R...  270 us
    reduce_sum x1, other arithmetic, local(): fine_grad.reshape(slab_depth // R, R, rows_count // R, R, cols_count // R...  80.2 us
    psum x1, waiting for transfers between devices, local(): summed = lax.psum(coarse, 'tracer')  46.6 us
    add x2, other arithmetic, local(): padded[1:-1]  39.1 us
  transfers between devices with their start and end apart: 13, of which 3 were waited for; matrix products, arithmetic and copies ran while one was open for 35% of the time, Pallas kernels for 0%

commit v1 on v0

v1 whole, which is shorter than its diff:
```python
import functools
import math

import jax
import jax.numpy as jnp
from jax import lax
from jax.experimental import pallas as pl
from jax.experimental.pallas import tpu as pltpu
from jax.sharding import PartitionSpec as P

R = 2
STEPS = 2
HALO = 2 * STEPS
STRIP = 64
LANES = 128

TIME_STEP = 0.14
PRIOR_RANGE = 4.0


def log2_of(size):
    bits = size.bit_length() - 1
    assert size == 1 << bits
    return bits


def sort_kernel(bits, key_in, value_in, keys, values):
    keys[...] = key_in[...]
    values[...] = value_in[...]
    blocks = keys.shape[0]
    group = min(8, blocks)

    def index_of(first, count):
        shape = (count, 8, LANES)
        return (
            (first + lax.broadcasted_iota(jnp.int32, shape, 0)) * (8 * LANES)
            + lax.broadcasted_iota(jnp.int32, shape, 1) * LANES
            + lax.broadcasted_iota(jnp.int32, shape, 2)
        )

    def far(distance, span):
        for first in range(0, blocks, 2 * distance):
            for start in range(first, first + distance, group):
                count = min(group, distance)
                low, high = pl.ds(start, count), pl.ds(start + distance, count)
                a, b, x, y = keys[low], keys[high], values[low], values[high]
                up = (index_of(start, count) & span) == 0
                swap = (up & (a > b)) | (jnp.logical_not(up) & (b > a))
                keys[low] = jnp.where(swap, b, a)
                keys[high] = jnp.where(swap, a, b)
                values[low] = jnp.where(swap, y, x)
                values[high] = jnp.where(swap, x, y)

    def near(axis, shift, bit, span):
        size = 8 if axis == 1 else LANES
        for start in range(0, blocks, group):
            part = pl.ds(start, group)
            a, x = keys[part], values[part]
            index = index_of(start, group)
            upper = (index & bit) != 0
            keep_min = ((index & span) == 0) != upper

            def partner(v):
                return jnp.where(
                    upper, pltpu.roll(v, shift, axis), pltpu.roll(v, size - shift, axis)
                )

            b, y = partner(a), partner(x)
            swap = (keep_min & (b < a)) | (jnp.logical_not(keep_min) & (b > a))
            keys[part] = jnp.where(swap, b, a)
            values[part] = jnp.where(swap, y, x)

    @pl.loop(0, bits)
    def _(phase):
        span = jnp.left_shift(jnp.int32(1), phase + 1)
        for q in reversed(range(bits)):

            @pl.when(q <= phase)
            def _():
                bit = 1 << q
                if bit >= 8 * LANES:
                    far(bit // (8 * LANES), span)
                elif bit >= LANES:
                    near(1, bit // LANES, bit, span)
                else:
                    near(2, bit, bit, span)


def sort_probes(keys, values):
    count = keys.shape[0]
    bits = log2_of(count)
    shape = (count // (8 * LANES), 8, LANES)
    spec = pl.BlockSpec(memory_space=pltpu.VMEM)
    keys, values = pl.pallas_call(
        functools.partial(sort_kernel, bits),
        out_shape=(
            jax.ShapeDtypeStruct(shape, jnp.int32),
            jax.ShapeDtypeStruct(shape, jnp.float32),
        ),
        in_specs=[spec, spec],
        out_specs=(spec, spec),
        cost_estimate=pl.CostEstimate(
            flops=count * 2000, bytes_accessed=count * 16, transcendentals=0
        ),
        name="sort_probes",
    )(keys.reshape(shape), values.reshape(shape))
    return keys.reshape(count // LANES, LANES), values.reshape(count // LANES, LANES)


def field_kernel(
    place,
    starts,
    keys,
    values,
    velocity,
    profile,
    rate_ref,
    rate_low,
    rate_high,
    init_ref,
    init_low,
    init_high,
    out,
    kappa,
    state0,
    state1,
    adjoint2,
    adjoint1,
    face_z,
    face_x,
    face_y,
    wind,
    counts,
    sums,
    sems,
):
    slab, rows, cols = rate_ref.shape
    planes = slab + 2 * HALO
    col_bits = log2_of(cols)
    row_bits = log2_of(rows)
    copies = []
    for number, (own, low, high, target) in enumerate(
        ((rate_ref, rate_low, rate_high, kappa), (init_ref, init_low, init_high, state0))
    ):
        for part, (source, first, count) in enumerate(
            ((own, HALO, slab), (low, 0, HALO), (high, HALO + slab, HALO))
        ):
            copy = pltpu.make_async_copy(
                source, target.at[pl.ds(first, count)], sems.at[3 * number + part]
            )
            copy.start()
            copies.append(copy)
    for copy in copies:
        copy.wait()

    starting = range(0, rows, STRIP)
    half = 0.5 * TIME_STEP

    def window(ref, z, r, after=True):
        pieces = [ref[z, pl.ds((r - 8) % rows, 8), :], ref[z, pl.ds(r, STRIP), :]]
        if after:
            pieces.append(ref[z, pl.ds((r + STRIP) % rows, 8), :])
        return jnp.concatenate(pieces, axis=0)

    def steps_down(wide):
        return (pltpu.roll(wide, wide.shape[0] - 1, 0) - wide)[: STRIP + 8]

    def with_previous(flux):
        return flux[8:], pltpu.roll(flux, 1, 0)[8:]

    def ahead(v):
        return pltpu.roll(v, cols - 1, 1)

    def behind(v):
        return pltpu.roll(v, 1, 1)

    @pl.loop(0, planes)
    def _(z):
        for r in starting:
            part = pl.ds(r, STRIP)
            kappa[z, part, :] = jnp.exp(kappa[z, part, :])

    @pl.loop(0, planes - 1)
    def _(z):
        for r in starting:
            part = pl.ds(r, STRIP)
            wide = window(kappa, z, r)
            k = wide[8 : 8 + STRIP]
            face_z[z, part, :] = half * (k + kappa[z + 1, part, :])
            face_x[z, part, :] = half * (k + pltpu.roll(wide, STRIP + 15, 0)[8 : 8 + STRIP])
            face_y[z, part, :] = half * (k + ahead(k))

    for r in starting:
        part = pl.ds(r, STRIP)
        wind[part, :] = TIME_STEP * velocity[part, :]

    def stepped(ref, z, r, forward):
        part = pl.ds(r, STRIP)
        wide = window(ref, z, r)
        v = wide[8 : 8 + STRIP]
        upper, lower = face_z[z, part, :], face_z[z - 1, part, :]
        if forward:
            lower = lower + wind[part, :]
        else:
            upper = upper + wind[part, :]
        total = upper * (ref[z + 1, part, :] - v) - lower * (v - ref[z - 1, part, :])
        flux, previous = with_previous(window(face_x, z, r, False) * steps_down(wide))
        total = total + (flux - previous)
        flux = face_y[z, part, :] * (ahead(v) - v)
        return v + (total + (flux - behind(flux)))

    source_plane = place[0]

    def forward(ref, z, r):
        scale = jnp.where(z == source_plane, jnp.float32(TIME_STEP), jnp.float32(0.0))
        return stepped(ref, z, r, True) + scale * profile[pl.ds(r, STRIP), :]

    @pl.loop(1, planes - 1)
    def _(z):
        for r in starting:
            state1[z, pl.ds(r, STRIP), :] = forward(state0, z, r)

    blocks = keys.shape[0]
    span = 2 * LANES
    lane_rows = lax.broadcasted_iota(jnp.int32, (rows, span), 0)
    lane_cols = lax.broadcasted_iota(jnp.int32, (cols, span), 0)

    def gather_plane(bucket):
        first, last = starts[bucket], starts[bucket + 1]
        block = first // LANES

        def partial(number):
            at = [jnp.minimum(number + i, blocks - 1) for i in range(2)]
            own = [
                jnp.right_shift(keys[pl.ds(at[i], 1), :], col_bits + row_bits)
                == jnp.where(number + i < blocks, bucket, -1)
                for i in range(2)
            ]
            key = [keys[pl.ds(i, 1), :] for i in at]
            row = jnp.concatenate(
                [
                    jnp.where(mine, jnp.right_shift(k, col_bits) & (rows - 1), -1)
                    for mine, k in zip(own, key)
                ],
                axis=1,
            )
            col = jnp.concatenate(key, axis=1) & (cols - 1)
            value = jnp.concatenate([values[pl.ds(i, 1), :] for i in at], axis=1)
            high = value.astype(jnp.bfloat16).astype(jnp.float32)
            rest = value - high
            row_hot = jnp.where(lane_rows == row, 1.0, 0.0).astype(jnp.bfloat16)
            col_hit = lane_cols == col

            def hot(v):
                return jnp.where(col_hit, v, 0.0).astype(jnp.bfloat16)

            def product(a, b):
                return lax.dot_general(
                    a, b, (((1,), (1,)), ((), ())), preferred_element_type=jnp.float32
                )

            return product(row_hot, hot(1.0)), product(
                jnp.concatenate([row_hot, row_hot], axis=1),
                jnp.concatenate([hot(high), hot(rest)], axis=1),
            )

        counts[...], sums[...] = partial(block)

        @pl.loop(1, jnp.maximum((last + span - 1 - block * LANES) // span, 1))
        def _(number):
            count, total = partial(block + 2 * number)
            counts[...] += count
            sums[...] += total

    @pl.loop(2, planes - 2)
    def _(z):
        gather_plane(planes + z)
        for r in starting:
            part = pl.ds(r, STRIP)
            adjoint2[z, part, :] = counts[part, :] * forward(state1, z, r) - sums[part, :]

    @pl.loop(3, planes - 3)
    def _(z):
        gather_plane(z)
        for r in starting:
            part = pl.ds(r, STRIP)
            inject = counts[part, :] * state1[z, part, :] - sums[part, :]
            adjoint1[z, part, :] = stepped(adjoint2, z, r, False) + inject

    fields = ((state1, adjoint2), (state0, adjoint1))

    def upward(z, part):
        return sum(
            (state[z + 1, part, :] - state[z, part, :])
            * (adjoint[z + 1, part, :] - adjoint[z, part, :])
            for state, adjoint in fields
        )

    def level(z, r):
        wide = [(window(state, z, r), window(adjoint, z, r)) for state, adjoint in fields]
        flux, previous = with_previous(sum(steps_down(c) * steps_down(m) for c, m in wide))
        total = flux + previous
        inner = [(c[8 : 8 + STRIP], m[8 : 8 + STRIP]) for c, m in wide]
        flux = sum((ahead(c) - c) * (ahead(m) - m) for c, m in inner)
        return total + (flux + behind(flux))

    def pool(length):
        shape = (length, length // R)
        fine = lax.broadcasted_iota(jnp.int32, shape, 0)
        coarse = lax.broadcasted_iota(jnp.int32, shape, 1)
        return jnp.where((fine >= coarse * R) & (fine < coarse * R + R), 1.0, 0.0)

    def exact(a, b, dims):
        return lax.dot_general(
            a,
            b,
            (dims, ((), ())),
            precision=lax.Precision.HIGHEST,
            preferred_element_type=jnp.float32,
        )

    @pl.loop(0, slab // R)
    def _(number):
        for r in starting:
            part = pl.ds(r, STRIP)
            both = jnp.zeros((STRIP, cols), jnp.float32)
            below = upward(HALO + number * R - 1, part)
            for layer in range(R):
                z = HALO + number * R + layer
                above = upward(z, part)
                both = both + kappa[z, part, :] * (level(z, r) + (below + above))
                below = above
            sums[part, :] = (-half) * both
        narrow = exact(sums[...], pool(cols), ((1,), (0,)))
        out[number] = exact(pool(rows), narrow, ((0,), (0,)))


def fields(place, starts, keys, values, velocity, profile, rates, inits):
    slab, rows, cols = rates[0].shape
    planes = slab + 2 * HALO
    smem = pl.BlockSpec(memory_space=pltpu.SMEM)
    vmem = pl.BlockSpec(memory_space=pltpu.VMEM)
    hbm = pl.BlockSpec(memory_space=pl.ANY)
    field = pltpu.VMEM((planes, rows, cols), jnp.float32)
    plane = pltpu.VMEM((rows, cols), jnp.float32)
    return pl.pallas_call(
        field_kernel,
        out_shape=jax.ShapeDtypeStruct((slab // R, rows // R, cols // R), jnp.float32),
        in_specs=[smem, smem] + [vmem] * 4 + [hbm] * 6,
        out_specs=vmem,
        scratch_shapes=[field] * 8 + [plane] * 3 + [pltpu.SemaphoreType.DMA((6,))],
        compiler_params=pltpu.CompilerParams(vmem_limit_bytes=60 * 1024 * 1024),
        cost_estimate=pl.CostEstimate(
            flops=planes * rows * cols * 200,
            bytes_accessed=planes * rows * cols * 8,
            transcendentals=planes * rows * cols,
        ),
        name="fields",
    )(place, starts, keys, values, velocity, profile, *rates, *inits)


def halos(array, axis, width):
    count, length = lax.axis_size(axis), array.shape[0]
    up = [(i, (i + 1) % count) for i in range(count)]
    down = [(j, i) for i, j in up]
    before = lax.ppermute(array[length - width :], axis, up)
    after = lax.ppermute(array[:width], axis, down)
    return array, before, after


def hartley(length, first_row, count):
    indices = first_row + lax.iota(jnp.int32, count)
    phases = indices[:, None] * lax.iota(jnp.int32, length)[None, :] % length
    angles = 2.0 * math.pi / length * phases.astype(jnp.float32)
    return jnp.cos(angles) + jnp.sin(angles)


def transform(table, values, axis_dim):
    forms = ("kj,jab->kab", "kj,ajb->akb", "kj,abj->abk")
    return jnp.einsum(
        forms[axis_dim],
        table,
        values,
        precision=lax.Precision.HIGHEST,
        preferred_element_type=jnp.float32,
    )


def symbol_part(length, first_row, count):
    indices = (first_row + lax.iota(jnp.int32, count)) % length
    angles = 2.0 * math.pi / length * indices.astype(jnp.float32)
    return 2.0 - 2.0 * jnp.cos(angles)


def local(log_rate, velocity, initial, profile, plane, depth, row, column, step_of, observed):
    slab, rows, cols = log_rate.shape
    domains, tracers = lax.axis_size("domain"), lax.axis_size("tracer")
    full = slab * domains
    planes = slab + 2 * HALO
    first = lax.axis_index("domain") * slab - HALO
    rates = halos(log_rate, "domain", HALO)
    inits = halos(initial[0], "domain", HALO)

    layer = (depth[0] - first + full) % full
    bucket = jnp.where(layer < planes, (step_of[0] - 1) * planes + layer, STEPS * planes)
    keys = bucket * (rows * cols) + row[0] * cols + column[0]
    edges = lax.iota(jnp.int32, STEPS * planes + 1)
    starts = jnp.sum((bucket[None, :] < edges[:, None]).astype(jnp.int32), axis=1)
    keys, values = sort_probes(keys, observed[0])
    place = (plane - first + full) % full

    coarse = fields(place, starts, keys, values, velocity, profile[0], rates, inits)

    x_size, y_size = coarse.shape[1:]
    z_size = full // R
    x_table = hartley(x_size, 0, x_size)
    y_table = hartley(y_size, 0, y_size)
    z_table = hartley(z_size, 0, z_size)
    x_share, y_share, x_block = x_size // tracers, y_size // tracers, x_size // domains

    spectral = transform(y_table, coarse, 2)
    spectral = jnp.swapaxes(spectral, 1, 2)
    parts = spectral.reshape(slab // R, tracers, y_share, x_size)
    parts = lax.all_to_all(parts, "tracer", split_axis=1, concat_axis=1, tiled=True)
    spectral = transform(x_table, parts.sum(axis=1), 2)
    spectral = spectral.reshape(slab // R, y_share, domains, x_block)
    spectral = jnp.moveaxis(spectral, 2, 0)
    spectral = lax.all_to_all(spectral, "domain", split_axis=0, concat_axis=0, tiled=True)
    columns = spectral.reshape(z_size, y_share * x_block)
    columns = jnp.dot(z_table, columns, precision=lax.Precision.HIGHEST)
    lam_z = symbol_part(z_size, 0, z_size)
    lam_y = symbol_part(y_size, lax.axis_index("tracer") * y_share, y_share)
    lam_x = symbol_part(x_size, lax.axis_index("domain") * x_block, x_block)
    lam = lam_z[:, None] + (lam_y[:, None] + lam_x[None, :]).reshape(1, -1)
    factor = 1.0 + PRIOR_RANGE * lam
    columns = columns * (1.0 / (factor * factor) / (x_size * y_size * z_size))
    columns = jnp.dot(z_table, columns, precision=lax.Precision.HIGHEST)
    columns = columns.reshape(domains, slab // R, y_share, x_block)
    columns = lax.all_to_all(columns, "domain", split_axis=0, concat_axis=0, tiled=True)
    columns = jnp.moveaxis(columns, 0, 2).reshape(slab // R, y_share, x_size)
    columns = transform(x_table, columns, 2)
    columns = columns.reshape(slab // R, y_share, tracers, x_share)
    columns = jnp.moveaxis(columns, 2, 0)
    columns = lax.all_to_all(columns, "tracer", split_axis=0, concat_axis=0, tiled=True)
    columns = jnp.moveaxis(columns, 0, 1).reshape(slab // R, y_size, x_share)
    return jnp.einsum(
        "kj,zjx->zxk",
        y_table,
        columns,
        precision=lax.Precision.HIGHEST,
        preferred_element_type=jnp.float32,
    )


def solution(mesh):
    return jax.shard_map(
        local,
        mesh=mesh,
        in_specs=(
            P("domain", None, None),
            P(),
            P("tracer", "domain", None, None),
            P("tracer", None, None),
            P("tracer"),
            P("tracer", None),
            P("tracer", None),
            P("tracer", None),
            P("tracer", None),
            P("tracer", None),
        ),
        out_specs=P("domain", "tracer", None),
        check_vma=False,
    )
```

time: 1850 us -> 167 us (0.09); the launches traced: 1820 us -> 167 us
  local copies, waits for them, and re-layouts: 1140 us -> 9.44 us
  other arithmetic: 548 us -> 6.9 us
  Pallas kernels: 0 us -> 80.9 us
  waiting for transfers between devices: 77.1 us -> 33.3 us
    gather x2 -> x0, local copies, waits for them, and re-layouts: 775 us -> none  [local(): values.reshape(-1)[flat]]
    scatter-add x2 -> x0, other arithmetic: 347 us -> none  [inject(): return empty.at[flat].add(jnp.where(probe_steps == section, residual, 0.0...]
    reshape x3 -> x5, local copies, waits for them, and re-layouts: 281 us -> 2.4 us  [the longest x1 0.83 us: local(): parts = spectral.reshape(slab // R, tracers, y_share, x_size)]
    pallas_call x0 -> x2, Pallas kernels: none -> 80.9 us  [the longest x1 57.6 us: fields(): pl.pallas_call(field_kernel, out_shape=jax.ShapeDtypeStruct((slab // R, r...]
    reduce_sum x1 -> x2, other arithmetic: 80.2 us -> 1.4 us  [the longest x1 1.36 us: local(): jnp.sum((bucket[None, :] < edges[:, None]).astype(jnp.int32), axis=1)]
    slice x34 -> x2, local copies, waits for them, and re-layouts: 65.2 us -> 3.04 us  [halos(): after = lax.ppermute(array[:width], axis, down)]
    add x5 -> x2, other arithmetic: 62.7 us -> 0.81 us  [the longest x1 0.74 us: local(): keys = bucket * (rows * cols) + row[0] * cols + column[0]]
    mul x4 -> x3, other arithmetic: 53.8 us -> 0.13 us  [the longest x1 0.11 us: local(): keys = bucket * (rows * cols) + row[0] * cols + column[0]]
  transfers between devices with their start and end apart: 13 -> 7, of which waited for: 3 -> 5; matrix products, arithmetic and copies ran while one was open for 35% -> 3% of each run, Pallas kernels for 0% -> 14%
where the time goes in v1:
time: 167 us
  Pallas kernels  80.9 us (48%)
  waiting for transfers between devices  33.3 us (20%)
  starting transfers between devices  20.7 us (12%)
  local copies, waits for them, and re-layouts  9.44 us (6%)
  blocking collectives  7.52 us (5%)
  matrix products  6.91 us (4%)
  other arithmetic  6.9 us (4%)
    pallas_call x1, Pallas kernels, fields(): pl.pallas_call(field_kernel, out_shape=jax.ShapeDtypeStruct((slab // R, r...  57.6 us
    pallas_call x1, Pallas kernels, sort_probes(): pl.pallas_call(functools.partial(sort_kernel, bits), out_shape=(jax.Shape...  23.4 us
    ppermute x2, waiting for transfers between devices, halos(): before = lax.ppermute(array[length - width:], axis, up)  11 us
    all_to_all x1, waiting for transfers between devices, local(): lax.all_to_all(parts, 'tracer', split_axis=1, concat_axis=1, tiled=True)  8.61 us
    ppermute x2, starting transfers between devices, halos(): after = lax.ppermute(array[:width], axis, down)  7.64 us
    all_to_all x1, blocking collectives, local(): lax.all_to_all(columns, 'tracer', split_axis=0, concat_axis=0, tiled=True)  7.52 us
    all_to_all x1, waiting for transfers between devices, local(): lax.all_to_all(columns, 'domain', split_axis=0, concat_axis=0, tiled=True)  6.7 us
    all_to_all x1, waiting for transfers between devices, local(): lax.all_to_all(spectral, 'domain', split_axis=0, concat_axis=0, tiled=True)  6.58 us
  transfers between devices with their start and end apart: 7, of which 5 were waited for; matrix products, arithmetic and copies ran while one was open for 3% of the time, Pallas kernels for 14%

profile of v1, /device:TPU:0, one launch (start us, length us, event | category | flops | bytes accessed | tf_op | source)
XLA Modules:
  0.0 166.6 jit_solution(5886673084842991017)
XLA Ops:
  0.0 1.9 %fusion.97 = (f32[4,256,256]{2,1,0:T(8,128)S(1)}, f32[4,256,256]{2,1,0:T(8,128)S(1)}) fusion(f32[16,256,256]{2,1,0:T(8,128)} %rate_ref.1), kind=kLoop, calls=%fused_computation.133 | loop fusion | bytes 4194304 | tf_op jit(solution)/shard_map/slice | solution.py:367
  2.4 4.1 %collective-permute-start.1 = (f32[4,256,256]{2,1,0:T(8,128)S(1)}, f32[4,256,256]{2,1,0:T(8,128)}, u32[]{:S(2)}, u32[]{:S(2)}) collective-permute-start(f32[4,256,256]{2,1,0:T(8,128)S(1)} %get-tuple-element.13), channel_id=1, source_target_pairs={{1,0},{2,1},{3,2},{4,3},{5,4},{6,5},{7,6},{0,7},{9,8},{10,9},{11,1... | collective-permute-start | bytes 3145736 | tf_op jit(solution)/shard_map/ppermute | solution.py:367
  6.5 1.1 slice_bitcast_fusion
  7.7 3.5 %collective-permute-start.3 = (f32[4,256,256]{2,1,0:T(8,128)S(1)}, f32[4,256,256]{2,1,0:T(8,128)}, u32[]{:S(2)}, u32[]{:S(2)}) collective-permute-start(f32[4,256,256]{2,1,0:T(8,128)S(1)} %get-tuple-element.11), channel_id=1, source_target_pairs={{1,0},{2,1},{3,2},{4,3},{5,4},{6,5},{7,6},{0,7},{9,8},{10,9},{11,1... | collective-permute-start | bytes 3145736 | tf_op jit(solution)/shard_map/ppermute | solution.py:367
  11.2 1.6 compare_select_fusion.2
  14.3 23.4 %sort_probes.1 = (s32[32,8,128]{2,1,0:T(8,128)}, f32[32,8,128]{2,1,0:T(8,128)}) custom-call(s32[32,8,128]{2,1,0:T(8,128)} %add_add_fusion.key_in, f32[32,8,128]{2,1,0:T(8,128)} %bitcast.78), custom_call_target="tpu_custom_call" | custom-call | flops 65536000 | bytes 524288 | tf_op jit(solution)/shard_map/sort_probes/pallas_call | solution.py:94
  37.7 1.4 convert_reduce_fusion.starts
  39.1 11.0 %collective-permute-done.2.init_low = f32[4,256,256]{2,1,0:T(8,128)} collective-permute-done((f32[4,256,256]{2,1,0:T(8,128)}, f32[4,256,256]{2,1,0:T(8,128)}, u32[]{:S(2)}, u32[]{:S(2)}) %collective-permute-start.2) | collective-permute-done | bytes 1048608 | tf_op jit(solution)/shard_map/ppermute | solution.py:366
  50.5 57.6 %fields.1 = f32[8,128,128]{2,1,0:T(8,128)} custom-call(s32[1]{0:T(128)S(6)} %select_n.93.place, s32[49]{0:T(128)} %convert_reduce_fusion.starts, s32[256,128]{1,0:T(8,128)} %bitcast.75, f32[256,128]{1,0:T(8,128)} %bitcast.76, f32[256,256]{1,0:T(8,128)} %velocity.1, f32[256,256]{1,0:T(8,128)} %bitcast.74, f32[16,256,256]{2,1,0:T(8,128)} %rate_ref.1, ...), custom_call_target="tpu_custom_call" | custom-call | flops 314572800 | bytes 12582912 | tf_op jit(solution)/shard_map/fields/pallas_call | solution.py:346
  108.1 1.9 %fusion.16 = f32[8,128,128]{1,2,0:T(8,128)S(1)} fusion(f32[8,128,128]{2,1,0:T(8,128)} %fields.1), kind=kOutput, calls=%fused_computation.42 | convolution fusion | flops 201572352 | bytes 1048576 | tf_op jit(solution)/shard_map/kj,abj->abk/dot_general | solution.py:380
  110.8 4.3 %all-to-all-start = ((f32[8,4,32,128]{3,2,0,1:T(8,128)}), f32[8,4,32,128]{3,2,0,1:T(8,128)S(1)}, u32[]{:S(2)}, u32[]{:S(2)}) async-start(f32[8,4,32,128]{3,2,0,1:T(8,128)} %copy.25), calls=%async_computation | async-start | bytes 1048576 | tf_op jit(solution)/shard_map/all_to_all | solution.py:424
  115.3 8.6 %all-to-all-done = f32[8,4,32,128]{3,2,0,1:T(8,128)S(1)} async-done(((f32[8,4,32,128]{3,2,0,1:T(8,128)}), f32[8,4,32,128]{3,2,0,1:T(8,128)S(1)}, u32[]{:S(2)}, u32[]{:S(2)}) %all-to-all-start) | async-done | bytes 524320 | tf_op jit(solution)/shard_map/all_to_all | solution.py:424
  124.0 1.0 convolution_bitcast_fusion.1
  125.9 4.8 %all-to-all-start.1 = ((f32[8,1,4096]{2,1,0:T(1,128)}), f32[8,1,4096]{2,1,0:T(1,128)S(1)}, u32[]{:S(2)}, u32[]{:S(2)}) async-start(f32[8,1,4096]{2,1,0:T(1,128)} %reshape.211), calls=%async_computation.1 | async-start | bytes 262144 | tf_op jit(solution)/shard_map/all_to_all | solution.py:428
  130.9 6.6 %all-to-all-done.1 = f32[8,1,4096]{2,1,0:T(1,128)S(1)} async-done(((f32[8,1,4096]{2,1,0:T(1,128)}), f32[8,1,4096]{2,1,0:T(1,128)S(1)}, u32[]{:S(2)}, u32[]{:S(2)}) %all-to-all-start.1) | async-done | bytes 131104 | tf_op jit(solution)/shard_map/all_to_all | solution.py:428
  138.1 0.9 reduce
  141.7 0.9 reshape.213
  142.6 3.4 %all-to-all-start.2 = ((f32[8,1,4096]{2,1,0:T(1,128)}), f32[8,1,4096]{2,1,0:T(1,128)S(1)}, u32[]{:S(2)}, u32[]{:S(2)}) async-start(f32[8,1,4096]{2,1,0:T(1,128)} %reshape.213), calls=%async_computation.2 | async-start | bytes 262144 | tf_op jit(solution)/shard_map/all_to_all | solution.py:439
  146.0 6.7 %all-to-all-done.2 = f32[8,1,4096]{2,1,0:T(1,128)S(1)} async-done(((f32[8,1,4096]{2,1,0:T(1,128)}), f32[8,1,4096]{2,1,0:T(1,128)S(1)}, u32[]{:S(2)}, u32[]{:S(2)}) %all-to-all-start.2) | async-done | bytes 131104 | tf_op jit(solution)/shard_map/all_to_all | solution.py:439
  152.7 0.9 reduce.1
  153.9 2.0 %convolution_bitcast_fusion = f32[4,8,32,32]{3,2,0,1:T(8,128)S(1)} fusion(f32[8,32,128,1]{1,2,3,0:T(8,128)S(1)} %bitcast.68, s32[4,32]{1,0:T(4,128)S(1)} %multiply_add_fusion.1), kind=kOutput, calls=%fused_computation.2 | convolution fusion | flops 50577408 | bytes 262656 | tf_op jit(solution)/shard_map/kj,abj->abk/dot_general | solution.py:380
  156.2 7.5 %all_to_all.20 = f32[4,1,8192]{2,1,0:T(1,128)S(1)} all-to-all(f32[4,1,8192]{2,1,0:T(1,128)S(1)} %reshape.215), channel_id=1, replica_groups=mesh['tracer'=4,'domain'=8] {'tracer'}, dimensions={0} | all-to-all | bytes 262144 | tf_op jit(solution)/shard_map/all_to_all | solution.py:444
  163.7 1.0 reduce.2
  165.4 1.2 fusion.14
  (40 shorter events, 8.4 us)
Async XLA Ops:
  0.0 6.5 %copy-start = (f32[1,16,256,256]{3,2,1,0:T(8,128)S(1)}, f32[1,16,256,256]{3,2,1,0:T(8,128)}, u32[]{:S(2)}) copy-start(f32[1,16,256,256]{3,2,1,0:T(8,128)} %param.12) | copy-start | bytes 12582916
  0.0 12.8 %copy-start.2 = (s32[1,32768]{1,0:T(1,128)S(1)}, s32[1,32768]{1,0:T(1,128)}, u32[]{:S(2)}) copy-start(s32[1,32768]{1,0:T(1,128)} %param.16) | copy-start | bytes 393220
  0.0 13.6 %copy-start.1 = (s32[1,32768]{1,0:T(1,128)S(1)}, s32[1,32768]{1,0:T(1,128)}, u32[]{:S(2)}) copy-start(s32[1,32768]{1,0:T(1,128)} %param.17) | copy-start | bytes 393220
  1.9 37.2 %collective-permute-start = (f32[4,256,256]{2,1,0:T(8,128)S(1)}, f32[4,256,256]{2,1,0:T(8,128)}, u32[]{:S(2)}, u32[]{:S(2)}) collective-permute-start(f32[4,256,256]{2,1,0:T(8,128)S(1)} %get-tuple-element.14), channel_id=1, source_target_pairs={{0,1},{1,2},{2,3},{3,4},{4,5},{5,6},{6,7},{7,0},{8,9},{9,10},{10,1... | collective-permute-start | bytes 3145736 | tf_op jit(solution)/shard_map/ppermute | solution.py:366
  2.4 36.7 %collective-permute-start.1 = (f32[4,256,256]{2,1,0:T(8,128)S(1)}, f32[4,256,256]{2,1,0:T(8,128)}, u32[]{:S(2)}, u32[]{:S(2)}) collective-permute-start(f32[4,256,256]{2,1,0:T(8,128)S(1)} %get-tuple-element.13), channel_id=1, source_target_pairs={{1,0},{2,1},{3,2},{4,3},{5,4},{6,5},{7,6},{0,7},{9,8},{10,9},{11,1... | collective-permute-start | bytes 3145736 | tf_op jit(solution)/shard_map/ppermute | solution.py:367
  7.7 42.4 %collective-permute-start.2 = (f32[4,256,256]{2,1,0:T(8,128)}, f32[4,256,256]{2,1,0:T(8,128)}, u32[]{:S(2)}, u32[]{:S(2)}) collective-permute-start(f32[4,256,256]{2,1,0:T(8,128)} %get-tuple-element.12), channel_id=1, source_target_pairs={{0,1},{1,2},{2,3},{3,4},{4,5},{5,6},{6,7},{7,0},{8,9},{9,10},{10,1... | collective-permute-start | bytes 3145736 | tf_op jit(solution)/shard_map/ppermute | solution.py:366
  7.7 42.8 %collective-permute-start.3 = (f32[4,256,256]{2,1,0:T(8,128)S(1)}, f32[4,256,256]{2,1,0:T(8,128)}, u32[]{:S(2)}, u32[]{:S(2)}) collective-permute-start(f32[4,256,256]{2,1,0:T(8,128)S(1)} %get-tuple-element.11), channel_id=1, source_target_pairs={{1,0},{2,1},{3,2},{4,3},{5,4},{6,5},{7,6},{0,7},{9,8},{10,9},{11,1... | collective-permute-start | bytes 3145736 | tf_op jit(solution)/shard_map/ppermute | solution.py:367
  110.8 13.1 %all-to-all-start = ((f32[8,4,32,128]{3,2,0,1:T(8,128)}), f32[8,4,32,128]{3,2,0,1:T(8,128)S(1)}, u32[]{:S(2)}, u32[]{:S(2)}) async-start(f32[8,4,32,128]{3,2,0,1:T(8,128)} %copy.25), calls=%async_computation | async-start | bytes 1048576 | tf_op jit(solution)/shard_map/all_to_all | solution.py:424
  125.9 11.6 %all-to-all-start.1 = ((f32[8,1,4096]{2,1,0:T(1,128)}), f32[8,1,4096]{2,1,0:T(1,128)S(1)}, u32[]{:S(2)}, u32[]{:S(2)}) async-start(f32[8,1,4096]{2,1,0:T(1,128)} %reshape.211), calls=%async_computation.1 | async-start | bytes 262144 | tf_op jit(solution)/shard_map/all_to_all | solution.py:428
  142.6 10.1 %all-to-all-start.2 = ((f32[8,1,4096]{2,1,0:T(1,128)}), f32[8,1,4096]{2,1,0:T(1,128)S(1)}, u32[]{:S(2)}, u32[]{:S(2)}) async-start(f32[8,1,4096]{2,1,0:T(1,128)} %reshape.213), calls=%async_computation.2 | async-start | bytes 262144 | tf_op jit(solution)/shard_map/all_to_all | solution.py:439

commit v2 on v1

--- a/solution.py
+++ b/solution.py
@@ -359,6 +359,185 @@
     )(place, starts, keys, values, velocity, profile, *rates, *inits)
 
 
+def tail_kernel(
+    domains,
+    tracers,
+    coarse,
+    weights,
+    x_table,
+    y_table,
+    z_table,
+    out,
+    send_sum,
+    recv_sum,
+    send_z,
+    recv_z,
+    send_back,
+    recv_back,
+    send_x,
+    recv_x,
+    sum_sems,
+    z_sems,
+    back_sems,
+    x_sems,
+):
+    depth, x_size, y_size = coarse.shape
+    y_share, x_share = y_size // tracers, x_size // tracers
+    y_own = y_share // domains
+    z_size = depth * domains
+    tracer, domain = lax.axis_index("tracer"), lax.axis_index("domain")
+
+    barrier = pltpu.get_barrier_semaphore()
+    for axis, me, count in (("tracer", tracer, tracers), ("domain", domain, domains)):
+        for i in range(1, count):
+            pl.semaphore_signal(
+                barrier,
+                inc=1,
+                device_id={axis: lax.rem(me + i, count)},
+                device_id_type=pl.DeviceIdType.MESH,
+            )
+    pl.semaphore_wait(barrier, tracers + domains - 2)
+
+    def exact(a, b, dims):
+        return lax.dot_general(
+            a,
+            b,
+            (dims, ((), ())),
+            precision=lax.Precision.HIGHEST,
+            preferred_element_type=jnp.float32,
+        )
+
+    def exchange(axis, me, count, source, target, sems):
+        copies = []
+        for i in range(1, count):
+            peer = lax.rem(me + i, count)
+            copy = pltpu.make_async_remote_copy(
+                src_ref=source(peer),
+                dst_ref=target(i, me),
+                send_sem=sems.at[0, i],
+                recv_sem=sems.at[1, i],
+                device_id={axis: peer},
+                device_id_type=pl.DeviceIdType.MESH,
+            )
+            copy.start()
+            copies.append(copy)
+        return copies
+
+    spectral = exact(y_table[...], coarse[...].reshape(depth * x_size, y_size), ((1,), (1,)))
+    for block in range(tracers):
+        send_sum[block] = spectral[block * y_share : (block + 1) * y_share]
+    first = exchange(
+        "tracer",
+        tracer,
+        tracers,
+        lambda peer: send_sum.at[peer],
+        lambda i, me: recv_sum.at[i],
+        sum_sems,
+    )
+    total = send_sum[tracer]
+    for i, copy in enumerate(first):
+        copy.wait_recv()
+        total = total + recv_sum[i + 1]
+
+    for z in range(depth):
+        send_z[:, z, :] = exact(
+            total[:, z * x_size : (z + 1) * x_size], x_table[...], ((1,), (0,))
+        )
+    second = exchange(
+        "domain",
+        domain,
+        domains,
+        lambda peer: send_z.at[pl.ds(peer * y_own, y_own)],
+        lambda i, me: recv_z.at[me],
+        z_sems,
+    )
+    recv_z[domain] = send_z[pl.ds(domain * y_own, y_own)]
+    for copy in second:
+        copy.wait_recv()
+
+    for k in range(y_own):
+        column = recv_z[:, k].reshape(z_size, x_size)
+        column = exact(z_table[...], column, ((1,), (0,))) * weights[k]
+        column = exact(z_table[...], column, ((1,), (0,)))
+        send_back[:, k] = column.reshape(domains, depth, x_size)
+    third = exchange(
+        "domain",
+        domain,
+        domains,
+        lambda peer: send_back.at[peer],
+        lambda i, me: recv_back.at[pl.ds(me * y_own, y_own)],
+        back_sems,
+    )
+    recv_back[pl.ds(domain * y_own, y_own)] = send_back[domain]
+    for copy in third:
+        copy.wait_recv()
+
+    spectral = jnp.concatenate([recv_back[:, z, :] for z in range(depth)], axis=0)
+    spectral = exact(x_table[...], spectral, ((1,), (1,)))
+    for block in range(tracers):
+        send_x[block] = spectral[block * x_share : (block + 1) * x_share]
+    fourth = exchange(
+        "tracer",
+        tracer,
+        tracers,
+        lambda peer: send_x.at[peer],
+        lambda i, me: recv_x.at[me],
+        x_sems,
+    )
+    recv_x[tracer] = send_x[tracer]
+    for copy in fourth:
+        copy.wait_recv()
+
+    for z in range(depth):
+        lanes = slice(z * y_share, (z + 1) * y_share)
+        row = jnp.concatenate([recv_x[i][:, lanes] for i in range(tracers)], axis=1)
+        out[z] = exact(row, y_table[...], ((1,), (0,)))
+    for copy in first + second + third + fourth:
+        copy.wait_send()
+
+
+def filtered(coarse, weights, x_table, y_table, z_table):
+    depth, x_size, y_size = coarse.shape
+    domains, tracers = lax.axis_size("domain"), lax.axis_size("tracer")
+    y_share, x_share = y_size // tracers, x_size // tracers
+    y_own = y_share // domains
+    vmem = pl.BlockSpec(memory_space=pltpu.VMEM)
+
+    def buffer(*shape):
+        return pltpu.VMEM(shape, jnp.float32)
+
+    def sems(count):
+        return pltpu.SemaphoreType.DMA((2, count))
+
+    return pl.pallas_call(
+        functools.partial(tail_kernel, domains, tracers),
+        out_shape=jax.ShapeDtypeStruct((depth, x_share, y_size), jnp.float32),
+        in_specs=[vmem] * 5,
+        out_specs=vmem,
+        scratch_shapes=[
+            buffer(tracers, y_share, depth * x_size),
+            buffer(tracers, y_share, depth * x_size),
+            buffer(y_share, depth, x_size),
+            buffer(domains, y_own, depth, x_size),
+            buffer(domains, y_own, depth, x_size),
+            buffer(y_share, depth, x_size),
+            buffer(tracers, x_share, depth * y_share),
+            buffer(tracers, x_share, depth * y_share),
+            sems(tracers),
+            sems(domains),
+            sems(domains),
+            sems(tracers),
+        ],
+        compiler_params=pltpu.CompilerParams(
+            collective_id=1, has_side_effects=True, vmem_limit_bytes=24 * 1024 * 1024
+        ),
+        cost_estimate=pl.CostEstimate(
+            flops=coarse.size * 3000, bytes_accessed=coarse.size * 8, transcendentals=0
+        ),
+        name="filtered",
+    )(coarse, weights, x_table, y_table, z_table)
+
+
 def halos(array, axis, width):
     count, length = lax.axis_size(axis), array.shape[0]
     up = [(i, (i + 1) % count) for i in range(count)]
@@ -373,17 +552,6 @@
     phases = indices[:, None] * lax.iota(jnp.int32, length)[None, :] % length
     angles = 2.0 * math.pi / length * phases.astype(jnp.float32)
     return jnp.cos(angles) + jnp.sin(angles)
-
-
-def transform(table, values, axis_dim):
-    forms = ("kj,jab->kab", "kj,ajb->akb", "kj,abj->abk")
-    return jnp.einsum(
-        forms[axis_dim],
-        table,
-        values,
-        precision=lax.Precision.HIGHEST,
-        preferred_element_type=jnp.float32,
-    )
 
 
 def symbol_part(length, first_row, count):
@@ -411,45 +579,18 @@
 
     coarse = fields(place, starts, keys, values, velocity, profile[0], rates, inits)
 
-    x_size, y_size = coarse.shape[1:]
-    z_size = full // R
-    x_table = hartley(x_size, 0, x_size)
-    y_table = hartley(y_size, 0, y_size)
-    z_table = hartley(z_size, 0, z_size)
-    x_share, y_share, x_block = x_size // tracers, y_size // tracers, x_size // domains
-
-    spectral = transform(y_table, coarse, 2)
-    spectral = jnp.swapaxes(spectral, 1, 2)
-    parts = spectral.reshape(slab // R, tracers, y_share, x_size)
-    parts = lax.all_to_all(parts, "tracer", split_axis=1, concat_axis=1, tiled=True)
-    spectral = transform(x_table, parts.sum(axis=1), 2)
-    spectral = spectral.reshape(slab // R, y_share, domains, x_block)
-    spectral = jnp.moveaxis(spectral, 2, 0)
-    spectral = lax.all_to_all(spectral, "domain", split_axis=0, concat_axis=0, tiled=True)
-    columns = spectral.reshape(z_size, y_share * x_block)
-    columns = jnp.dot(z_table, columns, precision=lax.Precision.HIGHEST)
-    lam_z = symbol_part(z_size, 0, z_size)
-    lam_y = symbol_part(y_size, lax.axis_index("tracer") * y_share, y_share)
-    lam_x = symbol_part(x_size, lax.axis_index("domain") * x_block, x_block)
-    lam = lam_z[:, None] + (lam_y[:, None] + lam_x[None, :]).reshape(1, -1)
+    x_size, y_size, z_size = rows // R, cols // R, full // R
+    y_own = y_size // (tracers * domains)
+    own_first = (lax.axis_index("tracer") * domains + lax.axis_index("domain")) * y_own
+    lam = (
+        symbol_part(y_size, own_first, y_own)[:, None, None]
+        + symbol_part(z_size, 0, z_size)[None, :, None]
+        + symbol_part(x_size, 0, x_size)[None, None, :]
+    )
     factor = 1.0 + PRIOR_RANGE * lam
-    columns = columns * (1.0 / (factor * factor) / (x_size * y_size * z_size))
-    columns = jnp.dot(z_table, columns, precision=lax.Precision.HIGHEST)
-    columns = columns.reshape(domains, slab // R, y_share, x_block)
-    columns = lax.all_to_all(columns, "domain", split_axis=0, concat_axis=0, tiled=True)
-    columns = jnp.moveaxis(columns, 0, 2).reshape(slab // R, y_share, x_size)
-    columns = transform(x_table, columns, 2)
-    columns = columns.reshape(slab // R, y_share, tracers, x_share)
-    columns = jnp.moveaxis(columns, 2, 0)
-    columns = lax.all_to_all(columns, "tracer", split_axis=0, concat_axis=0, tiled=True)
-    columns = jnp.moveaxis(columns, 0, 1).reshape(slab // R, y_size, x_share)
-    return jnp.einsum(
-        "kj,zjx->zxk",
-        y_table,
-        columns,
-        precision=lax.Precision.HIGHEST,
-        preferred_element_type=jnp.float32,
-    )
+    weights = 1.0 / (factor * factor) / (x_size * y_size * z_size)
+    tables = [hartley(size, 0, size) for size in (x_size, y_size, z_size)]
+    return filtered(coarse, weights, *tables)
 
 
 def solution(mesh):

time: 167 us -> 138 us (0.83)
  Pallas kernels: 80.9 us -> 110 us
  waiting for transfers between devices: 33.3 us -> 10.6 us
  starting transfers between devices: 20.7 us -> 8.16 us
  blocking collectives: 7.52 us -> 0 us
  matrix products: 6.91 us -> 0 us
  local copies, waits for them, and re-layouts: 9.44 us -> 4.64 us
  other arithmetic: 6.9 us -> 4.55 us
    pallas_call x0 -> x1, Pallas kernels: none -> 28.2 us  [filtered(): pl.pallas_call(functools.partial(tail_kernel, domains, tracers), out_shap...]
    all_to_all x3 -> x0, waiting for transfers between devices: 21.9 us -> none  [the longest x1 8.61 us: local(): lax.all_to_all(parts, 'tracer', split_axis=1, concat_axis=1, tiled=True)]
    all_to_all x3 -> x0, starting transfers between devices: 12.5 us -> none  [the longest x1 4.82 us: local(): lax.all_to_all(spectral, 'domain', split_axis=0, concat_axis=0, tiled=True)]
    all_to_all x1 -> x0, blocking collectives: 7.52 us -> none  [local(): lax.all_to_all(columns, 'tracer', split_axis=0, concat_axis=0, tiled=True)]
    dot_general x6 -> x0, matrix products: 6.91 us -> none  [the longest x3 4.89 us: transform(): jnp.einsum(forms[axis_dim], table, values, precision=lax.Precision.HIGHES...]
    all_to_all x3 -> x0, other arithmetic: 2.84 us -> none  [the longest x1 0.97 us: local(): lax.all_to_all(columns, 'tracer', split_axis=0, concat_axis=0, tiled=True)]
    reshape x5 -> x0, local copies, waits for them, and re-layouts: 2.4 us -> none  [the longest x1 0.83 us: local(): parts = spectral.reshape(slab // R, tracers, y_share, x_size)]
  transfers between devices with their start and end apart: 7 -> 4, of which waited for: 5 -> 2; matrix products, arithmetic and copies ran while one was open for 3% -> 4% of each run, Pallas kernels for 14% -> 17%
where the time goes in v2:
time: 138 us
  Pallas kernels  110 us (80%)
  waiting for transfers between devices  10.6 us (8%)
  starting transfers between devices  8.16 us (6%)
  local copies, waits for them, and re-layouts  4.64 us (3%)
  other arithmetic  4.55 us (3%)
    pallas_call x1, Pallas kernels, fields(): pl.pallas_call(field_kernel, out_shape=jax.ShapeDtypeStruct((slab // R, r...  57.9 us
    pallas_call x1, Pallas kernels, filtered(): pl.pallas_call(functools.partial(tail_kernel, domains, tracers), out_shap...  28.2 us
    pallas_call x1, Pallas kernels, sort_probes(): pl.pallas_call(functools.partial(sort_kernel, bits), out_shape=(jax.Shape...  23.4 us
    ppermute x2, waiting for transfers between devices, halos(): before = lax.ppermute(array[length - width:], axis, up)  10.2 us
    ppermute x2, starting transfers between devices, halos(): after = lax.ppermute(array[:width], axis, down)  7.64 us
    slice x2, local copies, waits for them, and re-layouts, halos(): after = lax.ppermute(array[:width], axis, down)  2.94 us
  transfers between devices with their start and end apart: 4, of which 2 were waited for; matrix products, arithmetic and copies ran while one was open for 4% of the time, Pallas kernels for 17%

profile of v2, /device:TPU:0, one launch (start us, length us, event | category | flops | bytes accessed | tf_op | source)
XLA Modules:
  0.0 138.3 jit_solution(11876717898094787289)
XLA Ops:
  0.0 1.8 %fusion.30 = (f32[4,256,256]{2,1,0:T(8,128)S(1)}, f32[4,256,256]{2,1,0:T(8,128)S(1)}) fusion(f32[16,256,256]{2,1,0:T(8,128)} %rate_ref.1), kind=kLoop, calls=%fused_computation.60 | loop fusion | bytes 4194304 | tf_op jit(solution)/shard_map/slice | solution.py:546
  1.8 0.5 collective-permute-start
  2.4 4.1 %collective-permute-start.1 = (f32[4,256,256]{2,1,0:T(8,128)S(1)}, f32[4,256,256]{2,1,0:T(8,128)}, u32[]{:S(2)}, u32[]{:S(2)}) collective-permute-start(f32[4,256,256]{2,1,0:T(8,128)S(1)} %get-tuple-element.13), channel_id=1, source_target_pairs={{1,0},{2,1},{3,2},{4,3},{5,4},{6,5},{7,6},{0,7},{9,8},{10,9},{11,1... | collective-permute-start | bytes 3145736 | tf_op jit(solution)/shard_map/ppermute | solution.py:546
  6.5 1.1 slice_bitcast_fusion
  7.6 0.0 collective-permute-start.2
  7.6 3.5 %collective-permute-start.3 = (f32[4,256,256]{2,1,0:T(8,128)S(1)}, f32[4,256,256]{2,1,0:T(8,128)}, u32[]{:S(2)}, u32[]{:S(2)}) collective-permute-start(f32[4,256,256]{2,1,0:T(8,128)S(1)} %get-tuple-element.11), channel_id=1, source_target_pairs={{1,0},{2,1},{3,2},{4,3},{5,4},{6,5},{7,6},{0,7},{9,8},{10,9},{11,1... | collective-permute-start | bytes 3145736 | tf_op jit(solution)/shard_map/ppermute | solution.py:546
  11.2 0.1 broadcast_multiply_fusion
  11.3 1.6 %compare_select_fusion.2 = (s32[1,32768]{1,0:T(1,128)S(1)}, s32[1,32768]{1,0:T(1,128)S(1)}, s32[1,32768]{1,0:T(1,128)S(1)}) fusion(s32[1,32768]{1,0:T(1,128)} %param.18, s32[1,32768]{1,0:T(1,128)} %param.15, s32[]{:T(128)} %sub.43), kind=kLoop, calls=%fused_computation.6 | loop fusion | flops 589824 | bytes 655364 | tf_op jit(solution)/shard_map/jit(_where)/select_n | solution.py:573
  12.9 0.7 add_add_fusion.key_in
  14.4 23.4 %sort_probes.1 = (s32[32,8,128]{2,1,0:T(8,128)}, f32[32,8,128]{2,1,0:T(8,128)}) custom-call(s32[32,8,128]{2,1,0:T(8,128)} %add_add_fusion.key_in, f32[32,8,128]{2,1,0:T(8,128)} %bitcast.24), custom_call_target="tpu_custom_call" | custom-call | flops 65536000 | bytes 524288 | tf_op jit(solution)/shard_map/sort_probes/pallas_call | solution.py:94
  37.8 0.1 fusion.18
  37.8 0.1 sine_add_fusion.1.z_table
  38.0 0.3 sine_add_fusion.x_table.y_table
  38.3 1.4 convert_reduce_fusion.starts
  39.6 0.1 broadcast_add_fusion
  39.7 0.1 divide_multiply_fusion.weights
  39.8 0.0 collective-permute-done.rate_low
  39.8 0.0 collective-permute-done.1.rate_high
  39.8 10.2 %collective-permute-done.2.init_low = f32[4,256,256]{2,1,0:T(8,128)} collective-permute-done((f32[4,256,256]{2,1,0:T(8,128)}, f32[4,256,256]{2,1,0:T(8,128)}, u32[]{:S(2)}, u32[]{:S(2)}) %collective-permute-start.2) | collective-permute-done | bytes 1048608 | tf_op jit(solution)/shard_map/ppermute | solution.py:545
  50.0 0.4 collective-permute-done.3.init_high
  50.4 57.9 %fields.1.coarse = f32[8,128,128]{2,1,0:T(8,128)} custom-call(s32[1]{0:T(128)S(6)} %select_n.71.place, s32[49]{0:T(128)} %convert_reduce_fusion.starts, s32[256,128]{1,0:T(8,128)} %bitcast.21, f32[256,128]{1,0:T(8,128)} %bitcast.22, f32[256,256]{1,0:T(8,128)} %velocity.1, f32[256,256]{1,0:T(8,128)} %bitcast.20, f32[16,256,256]{2,1,0:T(8,128)} %rate_ref.1, ...), custom_call_target="tpu_custom_call" | custom-call | flops 314572800 | bytes 12582912 | tf_op jit(solution)/shard_map/fields/pallas_call | solution.py:346
  108.3 1.0 copy-done
  109.4 28.2 %filtered.1 = f32[8,32,128]{2,1,0:T(8,128)S(1)} custom-call(f32[8,128,128]{2,1,0:T(8,128)S(1)} %copy-done, f32[4,64,128]{2,1,0:T(8,128)S(1)} %divide_multiply_fusion.weights, f32[128,128]{1,0:T(8,128)S(1)} %sine_add_fusion.x_table.y_table, f32[128,128]{1,0:T(8,128)S(1)} %sine_add_fusion.x_table.y_table, f32[64,64]{1,0:T(8,128)S(1)} %sine_add_fusion.1.z_table), custom_call_target="tpu_custom_call" | custom-call | flops 393216000 | bytes 1048576 | tf_op jit(solution)/shard_map/filtered/pallas_call | solution.py:512
  137.6 0.7 copy.13
  (9 shorter events, 0.1 us)
Async XLA Ops:
  0.0 6.5 %copy-start.1 = (f32[1,16,256,256]{3,2,1,0:T(8,128)S(1)}, f32[1,16,256,256]{3,2,1,0:T(8,128)}, u32[]{:S(2)}) copy-start(f32[1,16,256,256]{3,2,1,0:T(8,128)} %param.12) | copy-start | bytes 12582916
  0.0 11.2 %copy-start.3 = (s32[1,32768]{1,0:T(1,128)S(1)}, s32[1,32768]{1,0:T(1,128)}, u32[]{:S(2)}) copy-start(s32[1,32768]{1,0:T(1,128)} %param.16) | copy-start | bytes 393220
  0.0 12.9 %copy-start.2 = (s32[1,32768]{1,0:T(1,128)S(1)}, s32[1,32768]{1,0:T(1,128)}, u32[]{:S(2)}) copy-start(s32[1,32768]{1,0:T(1,128)} %param.17) | copy-start | bytes 393220
  1.8 38.0 %collective-permute-start = (f32[4,256,256]{2,1,0:T(8,128)S(1)}, f32[4,256,256]{2,1,0:T(8,128)}, u32[]{:S(2)}, u32[]{:S(2)}) collective-permute-start(f32[4,256,256]{2,1,0:T(8,128)S(1)} %get-tuple-element.14), channel_id=1, source_target_pairs={{0,1},{1,2},{2,3},{3,4},{4,5},{5,6},{6,7},{7,0},{8,9},{9,10},{10,1... | collective-permute-start | bytes 3145736 | tf_op jit(solution)/shard_map/ppermute | solution.py:545
  2.4 37.5 %collective-permute-start.1 = (f32[4,256,256]{2,1,0:T(8,128)S(1)}, f32[4,256,256]{2,1,0:T(8,128)}, u32[]{:S(2)}, u32[]{:S(2)}) collective-permute-start(f32[4,256,256]{2,1,0:T(8,128)S(1)} %get-tuple-element.13), channel_id=1, source_target_pairs={{1,0},{2,1},{3,2},{4,3},{5,4},{6,5},{7,6},{0,7},{9,8},{10,9},{11,1... | collective-permute-start | bytes 3145736 | tf_op jit(solution)/shard_map/ppermute | solution.py:546
  7.6 42.5 %collective-permute-start.2 = (f32[4,256,256]{2,1,0:T(8,128)}, f32[4,256,256]{2,1,0:T(8,128)}, u32[]{:S(2)}, u32[]{:S(2)}) collective-permute-start(f32[4,256,256]{2,1,0:T(8,128)} %get-tuple-element.12), channel_id=1, source_target_pairs={{0,1},{1,2},{2,3},{3,4},{4,5},{5,6},{6,7},{7,0},{8,9},{9,10},{10,1... | collective-permute-start | bytes 3145736 | tf_op jit(solution)/shard_map/ppermute | solution.py:545
  7.6 42.8 %collective-permute-start.3 = (f32[4,256,256]{2,1,0:T(8,128)S(1)}, f32[4,256,256]{2,1,0:T(8,128)}, u32[]{:S(2)}, u32[]{:S(2)}) collective-permute-start(f32[4,256,256]{2,1,0:T(8,128)S(1)} %get-tuple-element.11), channel_id=1, source_target_pairs={{1,0},{2,1},{3,2},{4,3},{5,4},{6,5},{7,6},{0,7},{9,8},{10,9},{11,1... | collective-permute-start | bytes 3145736 | tf_op jit(solution)/shard_map/ppermute | solution.py:546
  108.3 1.0 copy-start

commit v3 on v2

--- a/solution.py
+++ b/solution.py
@@ -13,6 +13,7 @@
 HALO = 2 * STEPS
 STRIP = 64
 LANES = 128
+AHEAD = 4
 
 TIME_STEP = 0.14
 PRIOR_RANGE = 4.0
@@ -107,11 +108,80 @@
     return keys.reshape(count // LANES, LANES), values.reshape(count // LANES, LANES)
 
 
+def bins_kernel(planes, row_bits, col_bits, starts, keys, values, out):
+    rows, cols = 1 << row_bits, 1 << col_bits
+    blocks = keys.shape[0]
+    span = 2 * LANES
+    number = pl.program_id(0)
+    bucket = jnp.where(number < planes - 4, planes + 2 + number, number - (planes - 4) + 3)
+    first, last = starts[bucket], starts[bucket + 1]
+    block = first // LANES
+    lane_rows = lax.broadcasted_iota(jnp.int32, (rows, span), 0)
+    lane_cols = lax.broadcasted_iota(jnp.int32, (cols, span), 0)
+
+    def partial(index):
+        at = [jnp.minimum(index + i, blocks - 1) for i in range(2)]
+        own = [
+            jnp.right_shift(keys[pl.ds(at[i], 1), :], col_bits + row_bits)
+            == jnp.where(index + i < blocks, bucket, -1)
+            for i in range(2)
+        ]
+        key = [keys[pl.ds(i, 1), :] for i in at]
+        row = jnp.concatenate(
+            [
+                jnp.where(mine, jnp.right_shift(k, col_bits) & (rows - 1), -1)
+                for mine, k in zip(own, key)
+            ],
+            axis=1,
+        )
+        col = jnp.concatenate(key, axis=1) & (cols - 1)
+        value = jnp.concatenate([values[pl.ds(i, 1), :] for i in at], axis=1)
+        high = value.astype(jnp.bfloat16).astype(jnp.float32)
+        rest = value - high
+        row_hot = jnp.where(lane_rows == row, 1.0, 0.0).astype(jnp.bfloat16)
+        col_hit = lane_cols == col
+
+        def hot(v):
+            return jnp.where(col_hit, v, 0.0).astype(jnp.bfloat16)
+
+        def product(a, b):
+            return lax.dot_general(
+                a, b, (((1,), (1,)), ((), ())), preferred_element_type=jnp.float32
+            )
+
+        return product(row_hot, hot(1.0)), product(
+            jnp.concatenate([row_hot, row_hot], axis=1),
+            jnp.concatenate([hot(high), hot(rest)], axis=1),
+        )
+
+    out[0, 0], out[0, 1] = partial(block)
+
+    @pl.loop(1, jnp.maximum((last + span - 1 - block * LANES) // span, 1))
+    def _(turn):
+        count, total = partial(block + 2 * turn)
+        out[0, 0] += count
+        out[0, 1] += total
+
+
+def bins(starts, keys, values, planes, rows, cols):
+    total = 2 * planes - 10
+    vmem = pl.BlockSpec(memory_space=pltpu.VMEM)
+    return pl.pallas_call(
+        functools.partial(bins_kernel, planes, log2_of(rows), log2_of(cols)),
+        grid=(total,),
+        out_shape=jax.ShapeDtypeStruct((total, 2, rows, cols), jnp.float32),
+        in_specs=[pl.BlockSpec(memory_space=pltpu.SMEM), vmem, vmem],
+        out_specs=pl.BlockSpec((1, 2, rows, cols), lambda i: (i, 0, 0, 0)),
+        compiler_params=pltpu.CompilerParams(vmem_limit_bytes=24 * 1024 * 1024),
+        cost_estimate=pl.CostEstimate(
+            flops=total * rows * cols * 1536, bytes_accessed=total * rows * cols * 8, transcendentals=0
+        ),
+        name="bins",
+    )(starts, keys, values)
+
+
 def field_kernel(
     place,
-    starts,
-    keys,
-    values,
     velocity,
     profile,
     rate_ref,
@@ -120,6 +190,7 @@
     init_ref,
     init_low,
     init_high,
+    probe_fields,
     out,
     kappa,
     state0,
@@ -130,14 +201,20 @@
     face_x,
     face_y,
     wind,
-    counts,
     sums,
+    injects,
     sems,
+    probe_sems,
 ):
     slab, rows, cols = rate_ref.shape
     planes = slab + 2 * HALO
-    col_bits = log2_of(cols)
-    row_bits = log2_of(rows)
+
+    def fetch(number):
+        slot = lax.rem(number, AHEAD)
+        return pltpu.make_async_copy(
+            probe_fields.at[number], injects.at[slot], probe_sems.at[slot]
+        )
+
     copies = []
     for number, (own, low, high, target) in enumerate(
         ((rate_ref, rate_low, rate_high, kappa), (init_ref, init_low, init_high, state0))
@@ -150,6 +227,8 @@
             )
             copy.start()
             copies.append(copy)
+    for number in range(AHEAD):
+        fetch(number).start()
     for copy in copies:
         copy.wait()
 
@@ -220,72 +299,34 @@
         for r in starting:
             state1[z, pl.ds(r, STRIP), :] = forward(state0, z, r)
 
-    blocks = keys.shape[0]
-    span = 2 * LANES
-    lane_rows = lax.broadcasted_iota(jnp.int32, (rows, span), 0)
-    lane_cols = lax.broadcasted_iota(jnp.int32, (cols, span), 0)
-
-    def gather_plane(bucket):
-        first, last = starts[bucket], starts[bucket + 1]
-        block = first // LANES
-
-        def partial(number):
-            at = [jnp.minimum(number + i, blocks - 1) for i in range(2)]
-            own = [
-                jnp.right_shift(keys[pl.ds(at[i], 1), :], col_bits + row_bits)
-                == jnp.where(number + i < blocks, bucket, -1)
-                for i in range(2)
-            ]
-            key = [keys[pl.ds(i, 1), :] for i in at]
-            row = jnp.concatenate(
-                [
-                    jnp.where(mine, jnp.right_shift(k, col_bits) & (rows - 1), -1)
-                    for mine, k in zip(own, key)
-                ],
-                axis=1,
-            )
-            col = jnp.concatenate(key, axis=1) & (cols - 1)
-            value = jnp.concatenate([values[pl.ds(i, 1), :] for i in at], axis=1)
-            high = value.astype(jnp.bfloat16).astype(jnp.float32)
-            rest = value - high
-            row_hot = jnp.where(lane_rows == row, 1.0, 0.0).astype(jnp.bfloat16)
-            col_hit = lane_cols == col
-
-            def hot(v):
-                return jnp.where(col_hit, v, 0.0).astype(jnp.bfloat16)
-
-            def product(a, b):
-                return lax.dot_general(
-                    a, b, (((1,), (1,)), ((), ())), preferred_element_type=jnp.float32
-                )
-
-            return product(row_hot, hot(1.0)), product(
-                jnp.concatenate([row_hot, row_hot], axis=1),
-                jnp.concatenate([hot(high), hot(rest)], axis=1),
-            )
-
-        counts[...], sums[...] = partial(block)
-
-        @pl.loop(1, jnp.maximum((last + span - 1 - block * LANES) // span, 1))
-        def _(number):
-            count, total = partial(block + 2 * number)
-            counts[...] += count
-            sums[...] += total
+    def probes(number):
+        fetch(number).wait()
+        return lax.rem(number, AHEAD)
+
+    def refill(number):
+        @pl.when(number + AHEAD < probe_fields.shape[0])
+        def _():
+            fetch(number + AHEAD).start()
 
     @pl.loop(2, planes - 2)
     def _(z):
-        gather_plane(planes + z)
+        number = z - 2
+        slot = probes(number)
         for r in starting:
             part = pl.ds(r, STRIP)
-            adjoint2[z, part, :] = counts[part, :] * forward(state1, z, r) - sums[part, :]
+            count, total = injects[slot, 0, part, :], injects[slot, 1, part, :]
+            adjoint2[z, part, :] = count * forward(state1, z, r) - total
+        refill(number)
 
     @pl.loop(3, planes - 3)
     def _(z):
-        gather_plane(z)
+        number = planes - 4 + z - 3
+        slot = probes(number)
         for r in starting:
             part = pl.ds(r, STRIP)
-            inject = counts[part, :] * state1[z, part, :] - sums[part, :]
+            inject = injects[slot, 0, part, :] * state1[z, part, :] - injects[slot, 1, part, :]
             adjoint1[z, part, :] = stepped(adjoint2, z, r, False) + inject
+        refill(number)
 
     fields = ((state1, adjoint2), (state0, adjoint1))
 
@@ -335,7 +376,7 @@
         out[number] = exact(pool(rows), narrow, ((0,), (0,)))
 
 
-def fields(place, starts, keys, values, velocity, profile, rates, inits):
+def fields(place, velocity, profile, rates, inits, probe_fields):
     slab, rows, cols = rates[0].shape
     planes = slab + 2 * HALO
     smem = pl.BlockSpec(memory_space=pltpu.SMEM)
@@ -346,9 +387,15 @@
     return pl.pallas_call(
         field_kernel,
         out_shape=jax.ShapeDtypeStruct((slab // R, rows // R, cols // R), jnp.float32),
-        in_specs=[smem, smem] + [vmem] * 4 + [hbm] * 6,
+        in_specs=[smem] + [vmem] * 2 + [hbm] * 7,
         out_specs=vmem,
-        scratch_shapes=[field] * 8 + [plane] * 3 + [pltpu.SemaphoreType.DMA((6,))],
+        scratch_shapes=[field] * 8
+        + [plane] * 2
+        + [
+            pltpu.VMEM((AHEAD, 2, rows, cols), jnp.float32),
+            pltpu.SemaphoreType.DMA((6,)),
+            pltpu.SemaphoreType.DMA((AHEAD,)),
+        ],
         compiler_params=pltpu.CompilerParams(vmem_limit_bytes=60 * 1024 * 1024),
         cost_estimate=pl.CostEstimate(
             flops=planes * rows * cols * 200,
@@ -356,7 +403,7 @@
             transcendentals=planes * rows * cols,
         ),
         name="fields",
-    )(place, starts, keys, values, velocity, profile, *rates, *inits)
+    )(place, velocity, profile, *rates, *inits, probe_fields)
 
 
 def tail_kernel(
@@ -577,7 +624,8 @@
     keys, values = sort_probes(keys, observed[0])
     place = (plane - first + full) % full
 
-    coarse = fields(place, starts, keys, values, velocity, profile[0], rates, inits)
+    probe_fields = bins(starts, keys, values, planes, rows, cols)
+    coarse = fields(place, velocity, profile[0], rates, inits, probe_fields)
 
     x_size, y_size, z_size = rows // R, cols // R, full // R
     y_own = y_size // (tracers * domains)

time: 138 us -> 140 us (1.014)
  local copies, waits for them, and re-layouts: 4.64 us -> 16.5 us
  waiting for transfers between devices: 10.6 us -> 0.01 us
    pallas_call x0 -> x1, Pallas kernels: none -> 13.4 us  [bins(): pl.pallas_call(functools.partial(bins_kernel, planes, log2_of(rows), log2...]
    pallas_call x1, Pallas kernels: 57.9 us -> 46.3 us  [fields(): pl.pallas_call(field_kernel, out_shape=jax.ShapeDtypeStruct((slab // R, r...]
    ppermute x2, waiting for transfers between devices: 10.2 us -> 0.01 us  [halos(): before = lax.ppermute(array[length - width:], axis, up)]
    unnamed x9 -> x19, local copies, waits for them, and re-layouts: 1.7 us -> 11.9 us
    pallas_call x1, Pallas kernels: 28.2 us -> 26 us  [filtered(): pl.pallas_call(functools.partial(tail_kernel, domains, tracers), out_shap...]
    slice x2, local copies, waits for them, and re-layouts: 2.94 us -> 4.66 us  [halos(): after = lax.ppermute(array[:width], axis, down)]
  transfers between devices with their start and end apart: 4 -> 4, of which waited for: 2 -> 0; matrix products, arithmetic and copies ran while one was open for 4% -> 5% of each run, Pallas kernels for 17% -> 26%
where the time goes in v3:
time: 140 us; the launch traced here: 139 us
  Pallas kernels  109 us (78%)
  local copies, waits for them, and re-layouts  16.5 us (12%)
  starting transfers between devices  8.03 us (6%)
  other arithmetic  4.94 us (4%)
    pallas_call x1, Pallas kernels, fields(): pl.pallas_call(field_kernel, out_shape=jax.ShapeDtypeStruct((slab // R, r...  46.3 us
    pallas_call x1, Pallas kernels, filtered(): pl.pallas_call(functools.partial(tail_kernel, domains, tracers), out_shap...  26 us
    pallas_call x1, Pallas kernels, sort_probes(): pl.pallas_call(functools.partial(sort_kernel, bits), out_shape=(jax.Shape...  23.4 us
    pallas_call x1, Pallas kernels, bins(): pl.pallas_call(functools.partial(bins_kernel, planes, log2_of(rows), log2...  13.4 us
    unnamed x19, local copies, waits for them, and re-layouts  11.9 us
    ppermute x2, starting transfers between devices, halos(): after = lax.ppermute(array[:width], axis, down)  7.58 us
    slice x2, local copies, waits for them, and re-layouts, halos(): after = lax.ppermute(array[:width], axis, down)  4.66 us
  transfers between devices with their start and end apart: 4, of which 0 were waited for; matrix products, arithmetic and copies ran while one was open for 5% of the time, Pallas kernels for 26%

profile of v3, /device:TPU:0, one launch (start us, length us, event | category | flops | bytes accessed | tf_op | source)
XLA Modules:
  0.0 139.4 jit_solution(11210278717961450771)
XLA Ops:
  0.0 3.2 %fusion.30 = (f32[4,256,256]{2,1,0:T(8,128)}, f32[4,256,256]{2,1,0:T(8,128)}) fusion(f32[16,256,256]{2,1,0:T(8,128)} %rate_ref.1), kind=kLoop, calls=%fused_computation.60 | loop fusion | bytes 4194304 | tf_op jit(solution)/shard_map/slice | solution.py:593
  3.2 0.5 collective-permute-start
  3.6 4.0 %collective-permute-start.1 = (f32[4,256,256]{2,1,0:T(8,128)}, f32[4,256,256]{2,1,0:T(8,128)S(1)}, u32[]{:S(2)}, u32[]{:S(2)}) collective-permute-start(f32[4,256,256]{2,1,0:T(8,128)} %get-tuple-element.13), channel_id=1, source_target_pairs={{1,0},{2,1},{3,2},{4,3},{5,4},{6,5},{7,6},{0,7},{9,8},{10,9},{11,1... | collective-permute-start | bytes 3145736 | tf_op jit(solution)/shard_map/ppermute | solution.py:593
  7.7 1.5 %slice_bitcast_fusion = (f32[4,256,256]{2,1,0:T(8,128)}, f32[4,256,256]{2,1,0:T(8,128)}) fusion(f32[1,16,256,256]{3,2,1,0:T(8,128)S(1)} %copy-done.4), kind=kLoop, calls=%fused_computation.2 | loop fusion | bytes 4194304 | tf_op jit(solution)/shard_map/slice | solution.py:593
  9.2 3.5 %collective-permute-start.3 = (f32[4,256,256]{2,1,0:T(8,128)}, f32[4,256,256]{2,1,0:T(8,128)}, u32[]{:S(2)}, u32[]{:S(2)}) collective-permute-start(f32[4,256,256]{2,1,0:T(8,128)} %get-tuple-element.11), channel_id=1, source_target_pairs={{1,0},{2,1},{3,2},{4,3},{5,4},{6,5},{7,6},{0,7},{9,8},{10,9},{11,1... | collective-permute-start | bytes 3145736 | tf_op jit(solution)/shard_map/ppermute | solution.py:593
  12.8 0.3 sine_add_fusion.x_table.y_table
  13.1 0.1 sine_add_fusion.1.z_table
  13.3 0.1 broadcast_multiply_fusion
  13.4 1.6 %compare_select_fusion.2 = (s32[1,32768]{1,0:T(1,128)S(1)}, s32[1,32768]{1,0:T(1,128)S(1)}, s32[1,32768]{1,0:T(1,128)S(1)}) fusion(s32[1,32768]{1,0:T(1,128)} %param.18, s32[1,32768]{1,0:T(1,128)} %param.15, s32[]{:T(128)} %sub.43), kind=kLoop, calls=%fused_computation.6 | loop fusion | flops 589824 | bytes 655364 | tf_op jit(solution)/shard_map/jit(_where)/select_n | solution.py:620
  15.0 1.6 %add_add_fusion.key_in = s32[32,8,128]{2,1,0:T(8,128)} fusion(s32[32,8,128]{2,1,0:T(8,128)} %bitcast.23, s32[32,8,128]{2,1,0:T(8,128)S(1)} %bitcast.18, s32[32,8,128]{2,1,0:T(8,128)S(1)} %bitcast.20, s32[32,8,128]{2,1,0:T(8,128)S(1)} %bitcast.19), kind=kLoop, calls=%fused_computation.14 | loop fusion | flops 557056 | bytes 655360 | tf_op jit(solution)/shard_map/add | solution.py:621
  17.3 23.4 %sort_probes.1 = (s32[32,8,128]{2,1,0:T(8,128)}, f32[32,8,128]{2,1,0:T(8,128)}) custom-call(s32[32,8,128]{2,1,0:T(8,128)} %add_add_fusion.key_in, f32[32,8,128]{2,1,0:T(8,128)} %bitcast.24), custom_call_target="tpu_custom_call" | custom-call | flops 65536000 | bytes 524288 | tf_op jit(solution)/shard_map/sort_probes/pallas_call | solution.py:95
  40.7 0.8 convert_reduce_fusion.starts
  41.6 0.1 divide_multiply_fusion.weights
  41.8 0.9 copy-done.2
  42.7 0.9 copy-done.3
  43.6 13.4 %bins.1.probe_fields = f32[38,2,256,256]{3,2,1,0:T(8,128)S(1)} custom-call(s32[49]{0:T(128)S(1)} %convert_reduce_fusion.starts, s32[256,128]{1,0:T(8,128)S(1)} %bitcast.15, f32[256,128]{1,0:T(8,128)S(1)} %bitcast.16), custom_call_target="tpu_custom_call" | custom-call | flops 3825205248 | bytes 19922944 | tf_op jit(solution)/shard_map/bins/pallas_call | solution.py:169
  57.0 6.7 %copy-done = f32[38,2,256,256]{3,2,1,0:T(8,128)} copy-done((f32[38,2,256,256]{3,2,1,0:T(8,128)}, f32[38,2,256,256]{3,2,1,0:T(8,128)S(1)}, u32[]{:S(2)}) %copy-start) | copy-done | bytes 19922968
  63.8 1.0 copy-done.5
  64.8 0.4 copy-done.6
  65.1 0.3 copy-done.7
  65.5 46.3 %fields.1.coarse = f32[8,128,128]{2,1,0:T(8,128)} custom-call(s32[1]{0:T(128)S(6)} %select_n.71.place, f32[256,256]{1,0:T(8,128)} %velocity.1, f32[256,256]{1,0:T(8,128)} %bitcast.22, f32[16,256,256]{2,1,0:T(8,128)} %rate_ref.1, f32[4,256,256]{2,1,0:T(8,128)} %copy-done.5, f32[4,256,256]{2,1,0:T(8,128)} %copy-done.6, f32[16,256,256]{2,1,0:T(8,128)} %bitcast.17, ...), custom_call_target="tpu_custom_call" | custom-call | flops 314572800 | bytes 12582912 | tf_op jit(solution)/shard_map/fields/pallas_call | solution.py:387
  111.8 1.0 copy-done.1
  112.8 26.0 %filtered.1 = f32[8,32,128]{2,1,0:T(8,128)S(1)} custom-call(f32[8,128,128]{2,1,0:T(8,128)S(1)} %copy-done.1, f32[4,64,128]{2,1,0:T(8,128)S(1)} %divide_multiply_fusion.weights, f32[128,128]{1,0:T(8,128)S(1)} %sine_add_fusion.x_table.y_table, f32[128,128]{1,0:T(8,128)S(1)} %sine_add_fusion.x_table.y_table, f32[64,64]{1,0:T(8,128)S(1)} %sine_add_fusion.1.z_table), custom_call_target="tpu_custom_call" | custom-call | flops 393216000 | bytes 1048576 | tf_op jit(solution)/shard_map/filtered/pallas_call | solution.py:559
  138.8 0.7 copy.13
  (20 shorter events, 0.2 us)
Async XLA Ops:
  0.0 7.7 %copy-start.4 = (f32[1,16,256,256]{3,2,1,0:T(8,128)S(1)}, f32[1,16,256,256]{3,2,1,0:T(8,128)}, u32[]{:S(2)}) copy-start(f32[1,16,256,256]{3,2,1,0:T(8,128)} %param.12) | copy-start | bytes 12582916
  0.0 13.2 %copy-start.8 = (s32[1,32768]{1,0:T(1,128)S(1)}, s32[1,32768]{1,0:T(1,128)}, u32[]{:S(2)}) copy-start(s32[1,32768]{1,0:T(1,128)} %param.16) | copy-start | bytes 393220
  3.2 60.6 %collective-permute-start = (f32[4,256,256]{2,1,0:T(8,128)}, f32[4,256,256]{2,1,0:T(8,128)S(1)}, u32[]{:S(2)}, u32[]{:S(2)}) collective-permute-start(f32[4,256,256]{2,1,0:T(8,128)} %get-tuple-element.14), channel_id=1, source_target_pairs={{0,1},{1,2},{2,3},{3,4},{4,5},{5,6},{6,7},{7,0},{8,9},{9,10},{10,1... | collective-permute-start | bytes 3145736 | tf_op jit(solution)/shard_map/ppermute | solution.py:592
  3.6 60.1 %collective-permute-start.1 = (f32[4,256,256]{2,1,0:T(8,128)}, f32[4,256,256]{2,1,0:T(8,128)S(1)}, u32[]{:S(2)}, u32[]{:S(2)}) collective-permute-start(f32[4,256,256]{2,1,0:T(8,128)} %get-tuple-element.13), channel_id=1, source_target_pairs={{1,0},{2,1},{3,2},{4,3},{5,4},{6,5},{7,6},{0,7},{9,8},{10,9},{11,1... | collective-permute-start | bytes 3145736 | tf_op jit(solution)/shard_map/ppermute | solution.py:593
  9.2 54.6 %collective-permute-start.2 = (f32[4,256,256]{2,1,0:T(8,128)}, f32[4,256,256]{2,1,0:T(8,128)S(1)}, u32[]{:S(2)}, u32[]{:S(2)}) collective-permute-start(f32[4,256,256]{2,1,0:T(8,128)} %get-tuple-element.12), channel_id=1, source_target_pairs={{0,1},{1,2},{2,3},{3,4},{4,5},{5,6},{6,7},{7,0},{8,9},{9,10},{10,1... | collective-permute-start | bytes 3145736 | tf_op jit(solution)/shard_map/ppermute | solution.py:592
  9.2 54.6 %collective-permute-start.3 = (f32[4,256,256]{2,1,0:T(8,128)}, f32[4,256,256]{2,1,0:T(8,128)}, u32[]{:S(2)}, u32[]{:S(2)}) collective-permute-start(f32[4,256,256]{2,1,0:T(8,128)} %get-tuple-element.11), channel_id=1, source_target_pairs={{1,0},{2,1},{3,2},{4,3},{5,4},{6,5},{7,6},{0,7},{9,8},{10,9},{11,1... | collective-permute-start | bytes 3145736 | tf_op jit(solution)/shard_map/ppermute | solution.py:593
  41.8 0.9 copy-start.2
  42.7 0.9 copy-start.3
  57.0 6.7 %copy-start = (f32[38,2,256,256]{3,2,1,0:T(8,128)}, f32[38,2,256,256]{3,2,1,0:T(8,128)S(1)}, u32[]{:S(2)}) copy-start(f32[38,2,256,256]{3,2,1,0:T(8,128)S(1)} %bins.1.probe_fields) | copy-start | bytes 59768836
  63.8 1.0 copy-start.5
  63.8 1.4 copy-start.6
  63.8 1.7 %copy-start.7 = (f32[4,256,256]{2,1,0:T(8,128)}, f32[4,256,256]{2,1,0:T(8,128)S(1)}, u32[]{:S(2)}) copy-start(f32[4,256,256]{2,1,0:T(8,128)S(1)} %collective-permute-done.2.init_low) | copy-start | bytes 3145732
  111.8 1.0 copy-start.1

commit v4 on v3

--- a/solution.py
+++ b/solution.py
@@ -14,6 +14,9 @@
 STRIP = 64
 LANES = 128
 AHEAD = 4
+SORT_BITS = 15
+BLOCKS = (1 << SORT_BITS) // (8 * LANES)
+VMEM_LIMIT = 60 * 1024 * 1024
 
 TIME_STEP = 0.14
 PRIOR_RANGE = 4.0
@@ -25,23 +28,45 @@
     return bits
 
 
-def sort_kernel(bits, key_in, value_in, keys, values):
-    keys[...] = key_in[...]
-    values[...] = value_in[...]
-    blocks = keys.shape[0]
-    group = min(8, blocks)
-
-    def index_of(first, count):
+def sort_kernel(
+    planes,
+    full,
+    shift_row,
+    shift_bucket,
+    first,
+    depth,
+    row,
+    column,
+    step,
+    observed,
+    keys_out,
+    values_out,
+    keys,
+    values,
+):
+    layer = depth[...] - first[0]
+    layer = jnp.where(layer < 0, layer + full, layer)
+    layer = jnp.where(layer >= full, layer - full, layer)
+    bucket = jnp.where(layer < planes, (step[...] - 1) * planes + layer, STEPS * planes)
+    keys[...] = (
+        jnp.left_shift(bucket, shift_bucket) | jnp.left_shift(row[...], shift_row) | column[...]
+    )
+    values[...] = observed[...]
+    group = 8
+
+    def index_of(start, count):
         shape = (count, 8, LANES)
+        major = start + lax.broadcasted_iota(jnp.int32, shape, 0)
         return (
-            (first + lax.broadcasted_iota(jnp.int32, shape, 0)) * (8 * LANES)
-            + lax.broadcasted_iota(jnp.int32, shape, 1) * LANES
-            + lax.broadcasted_iota(jnp.int32, shape, 2)
+            (major & 15)
+            | jnp.left_shift(lax.broadcasted_iota(jnp.int32, shape, 1), 4)
+            | jnp.left_shift(jnp.right_shift(major, 4), 7)
+            | jnp.left_shift(lax.broadcasted_iota(jnp.int32, shape, 2), 8)
         )
 
     def far(distance, span):
-        for first in range(0, blocks, 2 * distance):
-            for start in range(first, first + distance, group):
+        for begin in range(0, BLOCKS, 2 * distance):
+            for start in range(begin, begin + distance, group):
                 count = min(group, distance)
                 low, high = pl.ds(start, count), pl.ds(start + distance, count)
                 a, b, x, y = keys[low], keys[high], values[low], values[high]
@@ -54,7 +79,7 @@
 
     def near(axis, shift, bit, span):
         size = 8 if axis == 1 else LANES
-        for start in range(0, blocks, group):
+        for start in range(0, BLOCKS, group):
             part = pl.ds(start, group)
             a, x = keys[part], values[part]
             index = index_of(start, group)
@@ -71,46 +96,56 @@
             keys[part] = jnp.where(swap, b, a)
             values[part] = jnp.where(swap, y, x)
 
-    @pl.loop(0, bits)
+    @pl.loop(0, SORT_BITS)
     def _(phase):
         span = jnp.left_shift(jnp.int32(1), phase + 1)
-        for q in reversed(range(bits)):
+        for q in reversed(range(SORT_BITS)):
 
             @pl.when(q <= phase)
             def _():
                 bit = 1 << q
-                if bit >= 8 * LANES:
-                    far(bit // (8 * LANES), span)
-                elif bit >= LANES:
-                    near(1, bit // LANES, bit, span)
+                if q < 4:
+                    far(bit, span)
+                elif q == 7:
+                    far(16, span)
+                elif q < 7:
+                    near(1, bit >> 4, bit, span)
                 else:
-                    near(2, bit, bit, span)
-
-
-def sort_probes(keys, values):
-    count = keys.shape[0]
-    bits = log2_of(count)
-    shape = (count // (8 * LANES), 8, LANES)
-    spec = pl.BlockSpec(memory_space=pltpu.VMEM)
-    keys, values = pl.pallas_call(
-        functools.partial(sort_kernel, bits),
+                    near(2, bit >> 8, bit, span)
+
+    for half in range(2):
+        part = pl.ds(16 * half, 16)
+        keys_out[half] = keys[part].reshape(LANES, LANES).T
+        values_out[half] = values[part].reshape(LANES, LANES).T
+
+
+def sort_probes(first, planes, full, rows, cols, probes):
+    shape = (BLOCKS, 8, LANES)
+    assert probes[0].size == 1 << SORT_BITS
+    vmem = pl.BlockSpec(memory_space=pltpu.VMEM)
+    sizes = (2, LANES, LANES)
+    return pl.pallas_call(
+        functools.partial(
+            sort_kernel, planes, full, log2_of(cols), log2_of(rows) + log2_of(cols)
+        ),
         out_shape=(
-            jax.ShapeDtypeStruct(shape, jnp.int32),
-            jax.ShapeDtypeStruct(shape, jnp.float32),
-        ),
-        in_specs=[spec, spec],
-        out_specs=(spec, spec),
+            jax.ShapeDtypeStruct(sizes, jnp.int32),
+            jax.ShapeDtypeStruct(sizes, jnp.float32),
+        ),
+        in_specs=[pl.BlockSpec(memory_space=pltpu.SMEM)] + [vmem] * 5,
+        out_specs=(vmem, vmem),
+        scratch_shapes=[pltpu.VMEM(shape, jnp.int32), pltpu.VMEM(shape, jnp.float32)],
+        compiler_params=pltpu.CompilerParams(vmem_limit_bytes=VMEM_LIMIT),
         cost_estimate=pl.CostEstimate(
-            flops=count * 2000, bytes_accessed=count * 16, transcendentals=0
+            flops=2000 << SORT_BITS, bytes_accessed=28 << SORT_BITS, transcendentals=0
         ),
         name="sort_probes",
-    )(keys.reshape(shape), values.reshape(shape))
-    return keys.reshape(count // LANES, LANES), values.reshape(count // LANES, LANES)
+    )(first, *[array.reshape(shape) for array in probes])
 
 
 def bins_kernel(planes, row_bits, col_bits, starts, keys, values, out):
     rows, cols = 1 << row_bits, 1 << col_bits
-    blocks = keys.shape[0]
+    blocks = 2 * LANES
     span = 2 * LANES
     number = pl.program_id(0)
     bucket = jnp.where(number < planes - 4, planes + 2 + number, number - (planes - 4) + 3)
@@ -119,14 +154,17 @@
     lane_rows = lax.broadcasted_iota(jnp.int32, (rows, span), 0)
     lane_cols = lax.broadcasted_iota(jnp.int32, (cols, span), 0)
 
+    def chunk(ref, index):
+        return ref[index & 1, pl.ds(jnp.right_shift(index, 1), 1), :]
+
     def partial(index):
         at = [jnp.minimum(index + i, blocks - 1) for i in range(2)]
         own = [
-            jnp.right_shift(keys[pl.ds(at[i], 1), :], col_bits + row_bits)
+            jnp.right_shift(chunk(keys, at[i]), col_bits + row_bits)
             == jnp.where(index + i < blocks, bucket, -1)
             for i in range(2)
         ]
-        key = [keys[pl.ds(i, 1), :] for i in at]
+        key = [chunk(keys, i) for i in at]
         row = jnp.concatenate(
             [
                 jnp.where(mine, jnp.right_shift(k, col_bits) & (rows - 1), -1)
@@ -135,7 +173,7 @@
             axis=1,
         )
         col = jnp.concatenate(key, axis=1) & (cols - 1)
-        value = jnp.concatenate([values[pl.ds(i, 1), :] for i in at], axis=1)
+        value = jnp.concatenate([chunk(values, i) for i in at], axis=1)
         high = value.astype(jnp.bfloat16).astype(jnp.float32)
         rest = value - high
         row_hot = jnp.where(lane_rows == row, 1.0, 0.0).astype(jnp.bfloat16)
@@ -172,7 +210,7 @@
         out_shape=jax.ShapeDtypeStruct((total, 2, rows, cols), jnp.float32),
         in_specs=[pl.BlockSpec(memory_space=pltpu.SMEM), vmem, vmem],
         out_specs=pl.BlockSpec((1, 2, rows, cols), lambda i: (i, 0, 0, 0)),
-        compiler_params=pltpu.CompilerParams(vmem_limit_bytes=24 * 1024 * 1024),
+        compiler_params=pltpu.CompilerParams(vmem_limit_bytes=VMEM_LIMIT),
         cost_estimate=pl.CostEstimate(
             flops=total * rows * cols * 1536, bytes_accessed=total * rows * cols * 8, transcendentals=0
         ),
@@ -185,11 +223,9 @@
     velocity,
     profile,
     rate_ref,
-    rate_low,
-    rate_high,
     init_ref,
-    init_low,
-    init_high,
+    below,
+    above,
     probe_fields,
     out,
     kappa,
@@ -216,11 +252,13 @@
         )
 
     copies = []
-    for number, (own, low, high, target) in enumerate(
-        ((rate_ref, rate_low, rate_high, kappa), (init_ref, init_low, init_high, state0))
-    ):
+    for number, (own, target) in enumerate(((rate_ref, kappa), (init_ref, state0))):
         for part, (source, first, count) in enumerate(
-            ((own, HALO, slab), (low, 0, HALO), (high, HALO + slab, HALO))
+            (
+                (own, HALO, slab),
+                (below.at[number], 0, HALO),
+                (above.at[number], HALO + slab, HALO),
+            )
         ):
             copy = pltpu.make_async_copy(
                 source, target.at[pl.ds(first, count)], sems.at[3 * number + part]
@@ -376,18 +414,18 @@
         out[number] = exact(pool(rows), narrow, ((0,), (0,)))
 
 
-def fields(place, velocity, profile, rates, inits, probe_fields):
-    slab, rows, cols = rates[0].shape
+def fields(place, velocity, profile, rate, init, below, above, probe_fields):
+    slab, rows, cols = rate.shape
     planes = slab + 2 * HALO
     smem = pl.BlockSpec(memory_space=pltpu.SMEM)
     vmem = pl.BlockSpec(memory_space=pltpu.VMEM)
-    hbm = pl.BlockSpec(memory_space=pl.ANY)
+    anywhere = pl.BlockSpec(memory_space=pl.ANY)
     field = pltpu.VMEM((planes, rows, cols), jnp.float32)
     plane = pltpu.VMEM((rows, cols), jnp.float32)
     return pl.pallas_call(
         field_kernel,
         out_shape=jax.ShapeDtypeStruct((slab // R, rows // R, cols // R), jnp.float32),
-        in_specs=[smem] + [vmem] * 2 + [hbm] * 7,
+        in_specs=[smem] + [vmem] * 2 + [anywhere] * 5,
         out_specs=vmem,
         scratch_shapes=[field] * 8
         + [plane] * 2
@@ -396,14 +434,14 @@
             pltpu.SemaphoreType.DMA((6,)),
             pltpu.SemaphoreType.DMA((AHEAD,)),
         ],
-        compiler_params=pltpu.CompilerParams(vmem_limit_bytes=60 * 1024 * 1024),
+        compiler_params=pltpu.CompilerParams(vmem_limit_bytes=VMEM_LIMIT),
         cost_estimate=pl.CostEstimate(
             flops=planes * rows * cols * 200,
             bytes_accessed=planes * rows * cols * 8,
             transcendentals=planes * rows * cols,
         ),
         name="fields",
-    )(place, velocity, profile, *rates, *inits, probe_fields)
+    )(place, velocity, profile, rate, init, below, above, probe_fields)
 
 
 def tail_kernel(
@@ -576,7 +614,7 @@
             sems(tracers),
         ],
         compiler_params=pltpu.CompilerParams(
-            collective_id=1, has_side_effects=True, vmem_limit_bytes=24 * 1024 * 1024
+            collective_id=1, has_side_effects=True, vmem_limit_bytes=VMEM_LIMIT
         ),
         cost_estimate=pl.CostEstimate(
             flops=coarse.size * 3000, bytes_accessed=coarse.size * 8, transcendentals=0
@@ -585,13 +623,13 @@
     )(coarse, weights, x_table, y_table, z_table)
 
 
-def halos(array, axis, width):
-    count, length = lax.axis_size(axis), array.shape[0]
+def halos(arrays, axis, width):
+    count, length = lax.axis_size(axis), arrays[0].shape[0]
     up = [(i, (i + 1) % count) for i in range(count)]
     down = [(j, i) for i, j in up]
-    before = lax.ppermute(array[length - width :], axis, up)
-    after = lax.ppermute(array[:width], axis, down)
-    return array, before, after
+    last = jnp.stack([array[length - width :] for array in arrays])
+    initial = jnp.stack([array[:width] for array in arrays])
+    return lax.ppermute(last, axis, up), lax.ppermute(initial, axis, down)
 
 
 def hartley(length, first_row, count):
@@ -613,19 +651,17 @@
     full = slab * domains
     planes = slab + 2 * HALO
     first = lax.axis_index("domain") * slab - HALO
-    rates = halos(log_rate, "domain", HALO)
-    inits = halos(initial[0], "domain", HALO)
-
-    layer = (depth[0] - first + full) % full
-    bucket = jnp.where(layer < planes, (step_of[0] - 1) * planes + layer, STEPS * planes)
-    keys = bucket * (rows * cols) + row[0] * cols + column[0]
-    edges = lax.iota(jnp.int32, STEPS * planes + 1)
-    starts = jnp.sum((bucket[None, :] < edges[:, None]).astype(jnp.int32), axis=1)
-    keys, values = sort_probes(keys, observed[0])
+    below, above = halos((log_rate, initial[0]), "domain", HALO)
+
+    keys, values = sort_probes(
+        first.reshape(1), planes, full, rows, cols, (depth, row, column, step_of, observed)
+    )
+    edges = lax.iota(jnp.int32, STEPS * planes + 1) * (rows * cols)
+    starts = jnp.sum((keys[None] < edges[:, None, None, None]).astype(jnp.int32), axis=(1, 2, 3))
     place = (plane - first + full) % full
 
     probe_fields = bins(starts, keys, values, planes, rows, cols)
-    coarse = fields(place, velocity, profile[0], rates, inits, probe_fields)
+    coarse = fields(place, velocity, profile[0], log_rate, initial[0], below, above, probe_fields)
 
     x_size, y_size, z_size = rows // R, cols // R, full // R
     y_own = y_size // (tracers * domains)

time: 140 us -> 133 us (0.950)
  local copies, waits for them, and re-layouts: 16.5 us -> 5.89 us
  Pallas kernels: 109 us -> 113 us
  starting transfers between devices: 8.03 us -> 4.49 us
  other arithmetic: 4.94 us -> 8.28 us
    pallas_call x1, Pallas kernels: 13.4 us -> 23.3 us  [bins(): pl.pallas_call(functools.partial(bins_kernel, planes, log2_of(rows), log2...]
    pallas_call x1, Pallas kernels: 23.4 us -> 14.9 us  [sort_probes(): pl.pallas_call(functools.partial(sort_kernel, planes, full, log2_of(cols)...]
    unnamed x19 -> x5, local copies, waits for them, and re-layouts: 11.9 us -> 3.93 us
    ppermute x4 -> x2, starting transfers between devices: 8.03 us -> 4.49 us  [halos(): return (lax.ppermute(last, axis, up), lax.ppermute(initial, axis, down))]
    another operation x0 -> x2, other arithmetic: none -> 3.05 us  [the longest x1 1.53 us: halos(): last = jnp.stack([array[length - width:] for array in arrays])]
    slice x2 -> x1, local copies, waits for them, and re-layouts: 4.66 us -> 1.83 us  [halos(): initial = jnp.stack([array[:width] for array in arrays])]
    pallas_call x1, Pallas kernels: 26 us -> 28.4 us  [filtered(): pl.pallas_call(functools.partial(tail_kernel, domains, tracers), out_shap...]
    reduce_sum x1, other arithmetic: 0.84 us -> 2.56 us  [local(): jnp.sum((keys[None] < edges[:, None, None, None]).astype(jnp.int32), axis...]
  transfers between devices with their start and end apart: 4 -> 2, of which waited for: 0 -> 0; matrix products, arithmetic and copies ran while one was open for 5% -> 5% of each run, Pallas kernels for 26% -> 29%
where the time goes in v4:
time: 133 us; the launch traced here: 132 us
  Pallas kernels  113 us (85%)
  other arithmetic  8.28 us (6%)
  local copies, waits for them, and re-layouts  5.89 us (4%)
  starting transfers between devices  4.49 us (3%)
    pallas_call x1, Pallas kernels, fields(): pl.pallas_call(field_kernel, out_shape=jax.ShapeDtypeStruct((slab // R, r...  46.3 us
    pallas_call x1, Pallas kernels, filtered(): pl.pallas_call(functools.partial(tail_kernel, domains, tracers), out_shap...  28.4 us
    pallas_call x1, Pallas kernels, bins(): pl.pallas_call(functools.partial(bins_kernel, planes, log2_of(rows), log2...  23.3 us
    pallas_call x1, Pallas kernels, sort_probes(): pl.pallas_call(functools.partial(sort_kernel, planes, full, log2_of(cols)...  14.9 us
    ppermute x2, starting transfers between devices, halos(): return (lax.ppermute(last, axis, up), lax.ppermute(initial, axis, down))  4.49 us
    unnamed x5, local copies, waits for them, and re-layouts  3.93 us
  transfers between devices with their start and end apart: 2, of which 0 were waited for; matrix products, arithmetic and copies ran while one was open for 5% of the time, Pallas kernels for 29%

profile of v4, /device:TPU:0, one launch (start us, length us, event | category | flops | bytes accessed | tf_op | source)
XLA Modules:
  0.0 132.3 jit_solution(5578340443103227900)
XLA Ops:
  0.0 0.0 copy-start
  0.0 1.8 %fusion.28 = (f32[1,4,256,256]{3,2,1,0:T(8,128)S(1)}, f32[1,4,256,256]{3,2,1,0:T(8,128)S(1)}) fusion(f32[1,16,256,256]{3,2,1,0:T(8,128)} %param.12), kind=kLoop, calls=%fused_computation.49 | loop fusion | bytes 4194304 | tf_op jit(solution)/shard_map/slice | solution.py:631
  1.8 1.0 copy-done
  2.8 0.1 slice_bitcast_fusion
  3.0 1.5 %pad_maximum_fusion = f32[2,4,256,256]{3,2,1,0:T(8,128)} fusion(f32[1,4,256,256]{3,2,1,0:T(8,128)S(1)} %get-tuple-element.12, f32[1,4,256,256]{3,2,1,0:T(8,128)S(1)} %get-tuple-element.10), kind=kLoop, calls=%fused_computation.1 | loop fusion | flops 524288 | bytes 4194304 | tf_op jit(solution)/shard_map/stack | solution.py:630
  4.5 0.5 collective-permute-start
  4.9 1.5 %pad_maximum_fusion.1 = f32[2,4,256,256]{3,2,1,0:T(8,128)} fusion(f32[1,4,256,256]{3,2,1,0:T(8,128)S(1)} %get-tuple-element.11, f32[1,4,256,256]{3,2,1,0:T(8,128)S(1)} %get-tuple-element.9), kind=kLoop, calls=%fused_computation.2 | loop fusion | flops 524288 | bytes 4194304 | tf_op jit(solution)/shard_map/stack | solution.py:631
  6.5 4.0 %collective-permute-start.1 = (f32[2,4,256,256]{3,2,1,0:T(8,128)}, f32[2,4,256,256]{3,2,1,0:T(8,128)}, u32[]{:S(2)}, u32[]{:S(2)}) collective-permute-start(f32[2,4,256,256]{3,2,1,0:T(8,128)} %pad_maximum_fusion.1), channel_id=1, source_target_pairs={{1,0},{2,1},{3,2},{4,3},{5,4},{6,5},{7,6},{0,7},{9,8},{10,9},{11,1... | collective-permute-start | bytes 6291464 | tf_op jit(solution)/shard_map/ppermute | solution.py:632
  11.2 14.9 %sort_probes.1 = (s32[2,128,128]{2,1,0:T(8,128)}, f32[2,128,128]{2,1,0:T(8,128)}) custom-call(s32[1]{0:T(128)} %bitcast.first, s32[32,8,128]{2,1,0:T(8,128)} %bitcast.14, s32[32,8,128]{2,1,0:T(8,128)} %bitcast.15, s32[32,8,128]{2,1,0:T(8,128)} %bitcast.16, s32[32,8,128]{2,1,0:T(8,128)} %bitcast.17, f32[32,8,128]{2,1,0:T(8,128)} %bitcast.18), custom_call_target="tpu_custom_call" | custom-call | flops 65536000 | bytes 917504 | tf_op jit(solution)/shard_map/sort_probes/pallas_call | solution.py:127
  26.2 0.1 fusion.16
  26.3 0.8 sine_add_fusion.1.z_table
  27.1 0.9 sine_add_fusion.x_table.y_table
  28.0 2.6 %convert_reduce_fusion.starts = s32[49]{0:T(128)} fusion(s32[2,128,128]{2,1,0:T(8,128)} %get-tuple-element.7.keys, s32[49]{0:T(128)S(1)} %iota_multiply_fusion), kind=kLoop, calls=%fused_computation | loop fusion | flops 4816847 | bytes 131464 | tf_op jit(solution)/shard_map/reduce_sum | solution.py:660
  30.5 0.1 broadcast_add_fusion
  30.6 0.8 divide_multiply_fusion.weights
  31.4 23.3 %bins.1.probe_fields = f32[38,2,256,256]{3,2,1,0:T(8,128)} custom-call(s32[49]{0:T(128)} %convert_reduce_fusion.starts, s32[2,128,128]{2,1,0:T(8,128)} %get-tuple-element.7.keys, f32[2,128,128]{2,1,0:T(8,128)} %get-tuple-element.8.values), custom_call_target="tpu_custom_call" | custom-call | flops 3825205248 | bytes 19922944 | tf_op jit(solution)/shard_map/bins/pallas_call | solution.py:207
  54.6 0.0 collective-permute-done.below
  54.6 0.0 copy-start.1
  54.6 0.0 collective-permute-done.1.above
  54.6 1.4 %copy-done.1 = f32[2,4,256,256]{3,2,1,0:T(8,128)} copy-done((f32[2,4,256,256]{3,2,1,0:T(8,128)}, f32[2,4,256,256]{3,2,1,0:T(8,128)S(1)}, u32[]{:S(2)}) %copy-start.1) | copy-done | bytes 2097176
  56.0 46.3 %fields.1.coarse = f32[8,128,128]{2,1,0:T(8,128)} custom-call(s32[1]{0:T(128)S(6)} %select_n.53.place, f32[256,256]{1,0:T(8,128)} %velocity.1, f32[256,256]{1,0:T(8,128)} %bitcast.13, f32[16,256,256]{2,1,0:T(8,128)} %rate_ref.1, f32[16,256,256]{2,1,0:T(8,128)} %bitcast.12, f32[2,4,256,256]{3,2,1,0:T(8,128)} %copy-done.1, ...), custom_call_target="tpu_custom_call" | custom-call | flops 314572800 | bytes 12582912 | tf_op jit(solution)/shard_map/fields/pallas_call | solution.py:425
  102.3 28.4 %filtered.1 = f32[8,32,128]{2,1,0:T(8,128)} custom-call(f32[8,128,128]{2,1,0:T(8,128)} %fields.1.coarse, f32[4,64,128]{2,1,0:T(8,128)} %divide_multiply_fusion.weights, f32[128,128]{1,0:T(8,128)} %sine_add_fusion.x_table.y_table, f32[128,128]{1,0:T(8,128)} %sine_add_fusion.x_table.y_table, f32[64,64]{1,0:T(8,128)} %sine_add_fusion.1.z_table), custom_call_target="tpu_custom_call" | custom-call | flops 393216000 | bytes 1048576 | tf_op jit(solution)/shard_map/filtered/pallas_call | solution.py:597
  130.7 1.6 %copy.13 = f32[8,32,128]{2,1,0:T(8,128)} copy(f32[8,32,128]{2,1,0:T(8,128)} %filtered.1) | data formatting | bytes 262144
  (3 shorter events, 0.1 us)
Async XLA Ops:
  0.0 2.8 %copy-start = (f32[16,256,256]{2,1,0:T(8,128)S(1)}, f32[16,256,256]{2,1,0:T(8,128)}, u32[]{:S(2)}) copy-start(f32[16,256,256]{2,1,0:T(8,128)} %rate_ref.1) | copy-start | bytes 12582916
  4.5 50.1 %collective-permute-start = (f32[2,4,256,256]{3,2,1,0:T(8,128)}, f32[2,4,256,256]{3,2,1,0:T(8,128)S(1)}, u32[]{:S(2)}, u32[]{:S(2)}) collective-permute-start(f32[2,4,256,256]{3,2,1,0:T(8,128)} %pad_maximum_fusion), channel_id=1, source_target_pairs={{0,1},{1,2},{2,3},{3,4},{4,5},{5,6},{6,7},{7,0},{8,9},{9,10},{10,1... | collective-permute-start | bytes 6291464 | tf_op jit(solution)/shard_map/ppermute | solution.py:632
  6.5 48.2 %collective-permute-start.1 = (f32[2,4,256,256]{3,2,1,0:T(8,128)}, f32[2,4,256,256]{3,2,1,0:T(8,128)}, u32[]{:S(2)}, u32[]{:S(2)}) collective-permute-start(f32[2,4,256,256]{3,2,1,0:T(8,128)} %pad_maximum_fusion.1), channel_id=1, source_target_pairs={{1,0},{2,1},{3,2},{4,3},{5,4},{6,5},{7,6},{0,7},{9,8},{10,9},{11,1... | collective-permute-start | bytes 6291464 | tf_op jit(solution)/shard_map/ppermute | solution.py:632
  54.6 1.4 %copy-start.1 = (f32[2,4,256,256]{3,2,1,0:T(8,128)}, f32[2,4,256,256]{3,2,1,0:T(8,128)S(1)}, u32[]{:S(2)}) copy-start(f32[2,4,256,256]{3,2,1,0:T(8,128)S(1)} %collective-permute-done.below) | copy-start | bytes 6291460

commit v5 on v4

--- a/solution.py
+++ b/solution.py
@@ -11,7 +11,7 @@
 R = 2
 STEPS = 2
 HALO = 2 * STEPS
-STRIP = 64
+STRIP = 32
 LANES = 128
 AHEAD = 4
 SORT_BITS = 15
@@ -143,7 +143,7 @@
     )(first, *[array.reshape(shape) for array in probes])
 
 
-def bins_kernel(planes, row_bits, col_bits, starts, keys, values, out):
+def bins_kernel(planes, row_bits, col_bits, starts, keys, values, counts, sums):
     rows, cols = 1 << row_bits, 1 << col_bits
     blocks = 2 * LANES
     span = 2 * LANES
@@ -192,13 +192,13 @@
             jnp.concatenate([hot(high), hot(rest)], axis=1),
         )
 
-    out[0, 0], out[0, 1] = partial(block)
+    counts[0], sums[0] = partial(block)
 
     @pl.loop(1, jnp.maximum((last + span - 1 - block * LANES) // span, 1))
     def _(turn):
         count, total = partial(block + 2 * turn)
-        out[0, 0] += count
-        out[0, 1] += total
+        counts[0] += count
+        sums[0] += total
 
 
 def bins(starts, keys, values, planes, rows, cols):
@@ -207,9 +207,9 @@
     return pl.pallas_call(
         functools.partial(bins_kernel, planes, log2_of(rows), log2_of(cols)),
         grid=(total,),
-        out_shape=jax.ShapeDtypeStruct((total, 2, rows, cols), jnp.float32),
+        out_shape=(jax.ShapeDtypeStruct((total, rows, cols), jnp.float32),) * 2,
         in_specs=[pl.BlockSpec(memory_space=pltpu.SMEM), vmem, vmem],
-        out_specs=pl.BlockSpec((1, 2, rows, cols), lambda i: (i, 0, 0, 0)),
+        out_specs=(pl.BlockSpec((1, rows, cols), lambda i: (i, 0, 0)),) * 2,
         compiler_params=pltpu.CompilerParams(vmem_limit_bytes=VMEM_LIMIT),
         cost_estimate=pl.CostEstimate(
             flops=total * rows * cols * 1536, bytes_accessed=total * rows * cols * 8, transcendentals=0
@@ -226,7 +226,8 @@
     init_ref,
     below,
     above,
-    probe_fields,
+    count_fields,
+    sum_fields,
     out,
     kappa,
     state0,
@@ -247,9 +248,12 @@
 
     def fetch(number):
         slot = lax.rem(number, AHEAD)
-        return pltpu.make_async_copy(
-            probe_fields.at[number], injects.at[slot], probe_sems.at[slot]
-        )
+        return [
+            pltpu.make_async_copy(
+                source.at[number], injects.at[slot, i], probe_sems.at[slot, i]
+            )
+            for i, source in enumerate((count_fields, sum_fields))
+        ]
 
     copies = []
     for number, (own, target) in enumerate(((rate_ref, kappa), (init_ref, state0))):
@@ -266,8 +270,9 @@
             copy.start()
             copies.append(copy)
     for number in range(AHEAD):
-        fetch(number).start()
-    for copy in copies:
+        for copy in fetch(number):
+            copy.start()
+    for copy in copies[:3]:
         copy.wait()
 
     starting = range(0, rows, STRIP)
@@ -306,6 +311,9 @@
             face_z[z, part, :] = half * (k + kappa[z + 1, part, :])
             face_x[z, part, :] = half * (k + pltpu.roll(wide, STRIP + 15, 0)[8 : 8 + STRIP])
             face_y[z, part, :] = half * (k + ahead(k))
+
+    for copy in copies[3:]:
+        copy.wait()
 
     for r in starting:
         part = pl.ds(r, STRIP)
@@ -338,13 +346,15 @@
             state1[z, pl.ds(r, STRIP), :] = forward(state0, z, r)
 
     def probes(number):
-        fetch(number).wait()
+        for copy in fetch(number):
+            copy.wait()
         return lax.rem(number, AHEAD)
 
     def refill(number):
-        @pl.when(number + AHEAD < probe_fields.shape[0])
+        @pl.when(number + AHEAD < count_fields.shape[0])
         def _():
-            fetch(number + AHEAD).start()
+            for copy in fetch(number + AHEAD):
+                copy.start()
 
     @pl.loop(2, planes - 2)
     def _(z):
@@ -414,7 +424,7 @@
         out[number] = exact(pool(rows), narrow, ((0,), (0,)))
 
 
-def fields(place, velocity, profile, rate, init, below, above, probe_fields):
+def fields(place, velocity, profile, rate, init, below, above, counts, sums):
     slab, rows, cols = rate.shape
     planes = slab + 2 * HALO
     smem = pl.BlockSpec(memory_space=pltpu.SMEM)
@@ -425,14 +435,14 @@
     return pl.pallas_call(
         field_kernel,
         out_shape=jax.ShapeDtypeStruct((slab // R, rows // R, cols // R), jnp.float32),
-        in_specs=[smem] + [vmem] * 2 + [anywhere] * 5,
+        in_specs=[smem] + [vmem] * 2 + [anywhere] * 6,
         out_specs=vmem,
         scratch_shapes=[field] * 8
         + [plane] * 2
         + [
             pltpu.VMEM((AHEAD, 2, rows, cols), jnp.float32),
             pltpu.SemaphoreType.DMA((6,)),
-            pltpu.SemaphoreType.DMA((AHEAD,)),
+            pltpu.SemaphoreType.DMA((AHEAD, 2)),
         ],
         compiler_params=pltpu.CompilerParams(vmem_limit_bytes=VMEM_LIMIT),
         cost_estimate=pl.CostEstimate(
@@ -441,7 +451,7 @@
             transcendentals=planes * rows * cols,
         ),
         name="fields",
-    )(place, velocity, profile, rate, init, below, above, probe_fields)
+    )(place, velocity, profile, rate, init, below, above, counts, sums)
 
 
 def tail_kernel(
@@ -660,8 +670,8 @@
     starts = jnp.sum((keys[None] < edges[:, None, None, None]).astype(jnp.int32), axis=(1, 2, 3))
     place = (plane - first + full) % full
 
-    probe_fields = bins(starts, keys, values, planes, rows, cols)
-    coarse = fields(place, velocity, profile[0], log_rate, initial[0], below, above, probe_fields)
+    counts, sums = bins(starts, keys, values, planes, rows, cols)
+    coarse = fields(place, velocity, profile[0], log_rate, initial[0], below, above, counts, sums)
 
     x_size, y_size, z_size = rows // R, cols // R, full // R
     y_own = y_size // (tracers * domains)

time: 133 us -> 131 us (0.985)
  Pallas kernels: 113 us -> 111 us
    pallas_call x1, Pallas kernels: 46.3 us -> 44.5 us  [fields(): pl.pallas_call(field_kernel, out_shape=jax.ShapeDtypeStruct((slab // R, r...]
  transfers between devices with their start and end apart: 2 -> 2, of which waited for: 0 -> 0; matrix products, arithmetic and copies ran while one was open for 5% -> 5% of each run, Pallas kernels for 29% -> 30%
where the time goes in v5:
time: 131 us; the launch traced here: 130 us
  Pallas kernels  111 us (85%)
  other arithmetic  8.27 us (6%)
  local copies, waits for them, and re-layouts  5.88 us (4%)
  starting transfers between devices  4.49 us (3%)
    pallas_call x1, Pallas kernels, fields(): pl.pallas_call(field_kernel, out_shape=jax.ShapeDtypeStruct((slab // R, r...  44.5 us
    pallas_call x1, Pallas kernels, filtered(): pl.pallas_call(functools.partial(tail_kernel, domains, tracers), out_shap...  27.6 us
    pallas_call x1, Pallas kernels, bins(): pl.pallas_call(functools.partial(bins_kernel, planes, log2_of(rows), log2...  23.9 us
    pallas_call x1, Pallas kernels, sort_probes(): pl.pallas_call(functools.partial(sort_kernel, planes, full, log2_of(cols)...  14.9 us
    ppermute x2, starting transfers between devices, halos(): return (lax.ppermute(last, axis, up), lax.ppermute(initial, axis, down))  4.49 us
    unnamed x5, local copies, waits for them, and re-layouts  3.91 us
  transfers between devices with their start and end apart: 2, of which 0 were waited for; matrix products, arithmetic and copies ran while one was open for 5% of the time, Pallas kernels for 30%

profile of v5, /device:TPU:0, one launch (start us, length us, event | category | flops | bytes accessed | tf_op | source)
XLA Modules:
  0.0 130.3 jit_solution(8267403815767188720)
XLA Ops:
  0.0 0.0 copy-start
  0.0 1.8 %fusion.28 = (f32[1,4,256,256]{3,2,1,0:T(8,128)S(1)}, f32[1,4,256,256]{3,2,1,0:T(8,128)S(1)}) fusion(f32[1,16,256,256]{3,2,1,0:T(8,128)} %param.12), kind=kLoop, calls=%fused_computation.49 | loop fusion | bytes 4194304 | tf_op jit(solution)/shard_map/slice | solution.py:641
  1.8 1.0 copy-done
  2.8 0.1 slice_bitcast_fusion
  3.0 1.5 %pad_maximum_fusion = f32[2,4,256,256]{3,2,1,0:T(8,128)} fusion(f32[1,4,256,256]{3,2,1,0:T(8,128)S(1)} %get-tuple-element.16, f32[1,4,256,256]{3,2,1,0:T(8,128)S(1)} %get-tuple-element.14), kind=kLoop, calls=%fused_computation.1 | loop fusion | flops 524288 | bytes 4194304 | tf_op jit(solution)/shard_map/stack | solution.py:640
  4.5 0.5 collective-permute-start
  4.9 1.5 %pad_maximum_fusion.1 = f32[2,4,256,256]{3,2,1,0:T(8,128)} fusion(f32[1,4,256,256]{3,2,1,0:T(8,128)S(1)} %get-tuple-element.15, f32[1,4,256,256]{3,2,1,0:T(8,128)S(1)} %get-tuple-element.13), kind=kLoop, calls=%fused_computation.2 | loop fusion | flops 524288 | bytes 4194304 | tf_op jit(solution)/shard_map/stack | solution.py:641
  6.4 4.0 %collective-permute-start.1 = (f32[2,4,256,256]{3,2,1,0:T(8,128)}, f32[2,4,256,256]{3,2,1,0:T(8,128)}, u32[]{:S(2)}, u32[]{:S(2)}) collective-permute-start(f32[2,4,256,256]{3,2,1,0:T(8,128)} %pad_maximum_fusion.1), channel_id=1, source_target_pairs={{1,0},{2,1},{3,2},{4,3},{5,4},{6,5},{7,6},{0,7},{9,8},{10,9},{11,1... | collective-permute-start | bytes 6291464 | tf_op jit(solution)/shard_map/ppermute | solution.py:642
  11.2 14.9 %sort_probes.1 = (s32[2,128,128]{2,1,0:T(8,128)}, f32[2,128,128]{2,1,0:T(8,128)}) custom-call(s32[1]{0:T(128)} %bitcast.first, s32[32,8,128]{2,1,0:T(8,128)} %bitcast.14, s32[32,8,128]{2,1,0:T(8,128)} %bitcast.15, s32[32,8,128]{2,1,0:T(8,128)} %bitcast.16, s32[32,8,128]{2,1,0:T(8,128)} %bitcast.17, f32[32,8,128]{2,1,0:T(8,128)} %bitcast.18), custom_call_target="tpu_custom_call" | custom-call | flops 65536000 | bytes 917504 | tf_op jit(solution)/shard_map/sort_probes/pallas_call | solution.py:127
  26.2 0.1 fusion.16
  26.3 0.8 sine_add_fusion.1.z_table
  27.0 0.9 sine_add_fusion.x_table.y_table
  27.9 2.6 %convert_reduce_fusion.starts = s32[49]{0:T(128)} fusion(s32[2,128,128]{2,1,0:T(8,128)} %get-tuple-element.9.keys, s32[49]{0:T(128)S(1)} %iota_multiply_fusion), kind=kLoop, calls=%fused_computation | loop fusion | flops 4816847 | bytes 131464 | tf_op jit(solution)/shard_map/reduce_sum | solution.py:670
  30.5 0.1 broadcast_add_fusion
  30.6 0.8 divide_multiply_fusion.weights
  31.4 23.9 %bins.1 = (f32[38,256,256]{2,1,0:T(8,128)}, f32[38,256,256]{2,1,0:T(8,128)}) custom-call(s32[49]{0:T(128)} %convert_reduce_fusion.starts, s32[2,128,128]{2,1,0:T(8,128)} %get-tuple-element.9.keys, f32[2,128,128]{2,1,0:T(8,128)} %get-tuple-element.10.values), custom_call_target="tpu_custom_call" | custom-call | flops 3825205248 | bytes 19922944 | tf_op jit(solution)/shard_map/bins/pallas_call | solution.py:207
  55.3 0.0 collective-permute-done.below
  55.3 0.0 copy-start.1
  55.3 0.0 collective-permute-done.1.above
  55.3 1.4 %copy-done.1 = f32[2,4,256,256]{3,2,1,0:T(8,128)} copy-done((f32[2,4,256,256]{3,2,1,0:T(8,128)}, f32[2,4,256,256]{3,2,1,0:T(8,128)S(1)}, u32[]{:S(2)}) %copy-start.1) | copy-done | bytes 2097176
  56.6 44.5 %fields.1.coarse = f32[8,128,128]{2,1,0:T(8,128)} custom-call(s32[1]{0:T(128)S(6)} %select_n.53.place, f32[256,256]{1,0:T(8,128)} %velocity.1, f32[256,256]{1,0:T(8,128)} %bitcast.13, f32[16,256,256]{2,1,0:T(8,128)} %rate_ref.1, f32[16,256,256]{2,1,0:T(8,128)} %bitcast.12, f32[2,4,256,256]{3,2,1,0:T(8,128)} %copy-done.1, ...), custom_call_target="tpu_custom_call" | custom-call | flops 314572800 | bytes 12582912 | tf_op jit(solution)/shard_map/fields/pallas_call | solution.py:435
  101.2 27.6 %filtered.1 = f32[8,32,128]{2,1,0:T(8,128)} custom-call(f32[8,128,128]{2,1,0:T(8,128)} %fields.1.coarse, f32[4,64,128]{2,1,0:T(8,128)} %divide_multiply_fusion.weights, f32[128,128]{1,0:T(8,128)} %sine_add_fusion.x_table.y_table, f32[128,128]{1,0:T(8,128)} %sine_add_fusion.x_table.y_table, f32[64,64]{1,0:T(8,128)} %sine_add_fusion.1.z_table), custom_call_target="tpu_custom_call" | custom-call | flops 393216000 | bytes 1048576 | tf_op jit(solution)/shard_map/filtered/pallas_call | solution.py:607
  128.8 1.6 %copy.13 = f32[8,32,128]{2,1,0:T(8,128)} copy(f32[8,32,128]{2,1,0:T(8,128)} %filtered.1) | data formatting | bytes 262144
  (3 shorter events, 0.1 us)
Async XLA Ops:
  0.0 2.8 %copy-start = (f32[16,256,256]{2,1,0:T(8,128)S(1)}, f32[16,256,256]{2,1,0:T(8,128)}, u32[]{:S(2)}) copy-start(f32[16,256,256]{2,1,0:T(8,128)} %rate_ref.1) | copy-start | bytes 12582916
  4.5 50.8 %collective-permute-start = (f32[2,4,256,256]{3,2,1,0:T(8,128)}, f32[2,4,256,256]{3,2,1,0:T(8,128)S(1)}, u32[]{:S(2)}, u32[]{:S(2)}) collective-permute-start(f32[2,4,256,256]{3,2,1,0:T(8,128)} %pad_maximum_fusion), channel_id=1, source_target_pairs={{0,1},{1,2},{2,3},{3,4},{4,5},{5,6},{6,7},{7,0},{8,9},{9,10},{10,1... | collective-permute-start | bytes 6291464 | tf_op jit(solution)/shard_map/ppermute | solution.py:642
  6.4 48.8 %collective-permute-start.1 = (f32[2,4,256,256]{3,2,1,0:T(8,128)}, f32[2,4,256,256]{3,2,1,0:T(8,128)}, u32[]{:S(2)}, u32[]{:S(2)}) collective-permute-start(f32[2,4,256,256]{3,2,1,0:T(8,128)} %pad_maximum_fusion.1), channel_id=1, source_target_pairs={{1,0},{2,1},{3,2},{4,3},{5,4},{6,5},{7,6},{0,7},{9,8},{10,9},{11,1... | collective-permute-start | bytes 6291464 | tf_op jit(solution)/shard_map/ppermute | solution.py:642
  55.3 1.4 %copy-start.1 = (f32[2,4,256,256]{3,2,1,0:T(8,128)}, f32[2,4,256,256]{3,2,1,0:T(8,128)S(1)}, u32[]{:S(2)}) copy-start(f32[2,4,256,256]{3,2,1,0:T(8,128)S(1)} %collective-permute-done.below) | copy-start | bytes 6291460

commit v6 on v5

--- a/solution.py
+++ b/solution.py
@@ -239,6 +239,7 @@
     face_y,
     wind,
     sums,
+    narrow,
     injects,
     sems,
     probe_sems,
@@ -399,14 +400,7 @@
         coarse = lax.broadcasted_iota(jnp.int32, shape, 1)
         return jnp.where((fine >= coarse * R) & (fine < coarse * R + R), 1.0, 0.0)
 
-    def exact(a, b, dims):
-        return lax.dot_general(
-            a,
-            b,
-            (dims, ((), ())),
-            precision=lax.Precision.HIGHEST,
-            preferred_element_type=jnp.float32,
-        )
+    pairs = jnp.concatenate([pool(cols).astype(jnp.bfloat16)] * 3, axis=0)
 
     @pl.loop(0, slab // R)
     def _(number):
@@ -420,8 +414,17 @@
                 both = both + kappa[z, part, :] * (level(z, r) + (below + above))
                 below = above
             sums[part, :] = (-half) * both
-        narrow = exact(sums[...], pool(cols), ((1,), (0,)))
-        out[number] = exact(pool(rows), narrow, ((0,), (0,)))
+        whole = sums[...]
+        high = whole.astype(jnp.bfloat16)
+        rest = whole - high.astype(jnp.float32)
+        middle = rest.astype(jnp.bfloat16)
+        low = (rest - middle.astype(jnp.float32)).astype(jnp.bfloat16)
+        narrow[...] = jnp.dot(
+            jnp.concatenate([high, middle, low], axis=1),
+            pairs,
+            preferred_element_type=jnp.float32,
+        )
+        out[number] = sum(narrow[pl.ds(i, rows // R, stride=R), :] for i in range(R))
 
 
 def fields(place, velocity, profile, rate, init, below, above, counts, sums):
@@ -440,6 +443,7 @@
         scratch_shapes=[field] * 8
         + [plane] * 2
         + [
+            pltpu.VMEM((rows, cols // R), jnp.float32),
             pltpu.VMEM((AHEAD, 2, rows, cols), jnp.float32),
             pltpu.SemaphoreType.DMA((6,)),
             pltpu.SemaphoreType.DMA((AHEAD, 2)),

time: 131 us -> 130 us (level)
  no operation moved by 1% of the time
where the time goes in v6:
time: 130 us
  Pallas kernels  111 us (85%)
  other arithmetic  8.27 us (6%)
  local copies, waits for them, and re-layouts  5.88 us (5%)
  starting transfers between devices  4.49 us (3%)
    pallas_call x1, Pallas kernels, fields(): pl.pallas_call(field_kernel, out_shape=jax.ShapeDtypeStruct((slab // R, r...  43.6 us
    pallas_call x1, Pallas kernels, filtered(): pl.pallas_call(functools.partial(tail_kernel, domains, tracers), out_shap...  28.1 us
    pallas_call x1, Pallas kernels, bins(): pl.pallas_call(functools.partial(bins_kernel, planes, log2_of(rows), log2...  23.9 us
    pallas_call x1, Pallas kernels, sort_probes(): pl.pallas_call(functools.partial(sort_kernel, planes, full, log2_of(cols)...  14.9 us
    ppermute x2, starting transfers between devices, halos(): return (lax.ppermute(last, axis, up), lax.ppermute(initial, axis, down))  4.49 us
    unnamed x5, local copies, waits for them, and re-layouts  3.91 us
  transfers between devices with their start and end apart: 2, of which 0 were waited for; matrix products, arithmetic and copies ran while one was open for 5% of the time, Pallas kernels for 30%

profile of v6, /device:TPU:0, one launch (start us, length us, event | category | flops | bytes accessed | tf_op | source)
XLA Modules:
  0.0 129.9 jit_solution(3064604259987787726)
XLA Ops:
  0.0 0.0 copy-start
  0.0 1.8 %fusion.28 = (f32[1,4,256,256]{3,2,1,0:T(8,128)S(1)}, f32[1,4,256,256]{3,2,1,0:T(8,128)S(1)}) fusion(f32[1,16,256,256]{3,2,1,0:T(8,128)} %param.12), kind=kLoop, calls=%fused_computation.49 | loop fusion | bytes 4194304 | tf_op jit(solution)/shard_map/slice | solution.py:645
  1.8 1.0 copy-done
  2.8 0.1 slice_bitcast_fusion
  3.0 1.5 %pad_maximum_fusion = f32[2,4,256,256]{3,2,1,0:T(8,128)} fusion(f32[1,4,256,256]{3,2,1,0:T(8,128)S(1)} %get-tuple-element.16, f32[1,4,256,256]{3,2,1,0:T(8,128)S(1)} %get-tuple-element.14), kind=kLoop, calls=%fused_computation.1 | loop fusion | flops 524288 | bytes 4194304 | tf_op jit(solution)/shard_map/stack | solution.py:644
  4.5 0.5 collective-permute-start
  4.9 1.5 %pad_maximum_fusion.1 = f32[2,4,256,256]{3,2,1,0:T(8,128)} fusion(f32[1,4,256,256]{3,2,1,0:T(8,128)S(1)} %get-tuple-element.15, f32[1,4,256,256]{3,2,1,0:T(8,128)S(1)} %get-tuple-element.13), kind=kLoop, calls=%fused_computation.2 | loop fusion | flops 524288 | bytes 4194304 | tf_op jit(solution)/shard_map/stack | solution.py:645
  6.4 4.0 %collective-permute-start.1 = (f32[2,4,256,256]{3,2,1,0:T(8,128)}, f32[2,4,256,256]{3,2,1,0:T(8,128)}, u32[]{:S(2)}, u32[]{:S(2)}) collective-permute-start(f32[2,4,256,256]{3,2,1,0:T(8,128)} %pad_maximum_fusion.1), channel_id=1, source_target_pairs={{1,0},{2,1},{3,2},{4,3},{5,4},{6,5},{7,6},{0,7},{9,8},{10,9},{11,1... | collective-permute-start | bytes 6291464 | tf_op jit(solution)/shard_map/ppermute | solution.py:646
  11.2 14.9 %sort_probes.1 = (s32[2,128,128]{2,1,0:T(8,128)}, f32[2,128,128]{2,1,0:T(8,128)}) custom-call(s32[1]{0:T(128)} %bitcast.first, s32[32,8,128]{2,1,0:T(8,128)} %bitcast.14, s32[32,8,128]{2,1,0:T(8,128)} %bitcast.15, s32[32,8,128]{2,1,0:T(8,128)} %bitcast.16, s32[32,8,128]{2,1,0:T(8,128)} %bitcast.17, f32[32,8,128]{2,1,0:T(8,128)} %bitcast.18), custom_call_target="tpu_custom_call" | custom-call | flops 65536000 | bytes 917504 | tf_op jit(solution)/shard_map/sort_probes/pallas_call | solution.py:127
  26.2 0.1 fusion.16
  26.3 0.8 sine_add_fusion.1.z_table
  27.0 0.9 sine_add_fusion.x_table.y_table
  27.9 2.6 %convert_reduce_fusion.starts = s32[49]{0:T(128)} fusion(s32[2,128,128]{2,1,0:T(8,128)} %get-tuple-element.9.keys, s32[49]{0:T(128)S(1)} %iota_multiply_fusion), kind=kLoop, calls=%fused_computation | loop fusion | flops 4816847 | bytes 131464 | tf_op jit(solution)/shard_map/reduce_sum | solution.py:674
  30.5 0.1 broadcast_add_fusion
  30.6 0.8 divide_multiply_fusion.weights
  31.4 23.9 %bins.1 = (f32[38,256,256]{2,1,0:T(8,128)}, f32[38,256,256]{2,1,0:T(8,128)}) custom-call(s32[49]{0:T(128)} %convert_reduce_fusion.starts, s32[2,128,128]{2,1,0:T(8,128)} %get-tuple-element.9.keys, f32[2,128,128]{2,1,0:T(8,128)} %get-tuple-element.10.values), custom_call_target="tpu_custom_call" | custom-call | flops 3825205248 | bytes 19922944 | tf_op jit(solution)/shard_map/bins/pallas_call | solution.py:207
  55.2 0.0 collective-permute-done.below
  55.2 0.0 copy-start.1
  55.3 0.0 collective-permute-done.1.above
  55.3 1.4 %copy-done.1 = f32[2,4,256,256]{3,2,1,0:T(8,128)} copy-done((f32[2,4,256,256]{3,2,1,0:T(8,128)}, f32[2,4,256,256]{3,2,1,0:T(8,128)S(1)}, u32[]{:S(2)}) %copy-start.1) | copy-done | bytes 2097176
  56.6 43.6 %fields.1.coarse = f32[8,128,128]{2,1,0:T(8,128)} custom-call(s32[1]{0:T(128)S(6)} %select_n.53.place, f32[256,256]{1,0:T(8,128)} %velocity.1, f32[256,256]{1,0:T(8,128)} %bitcast.13, f32[16,256,256]{2,1,0:T(8,128)} %rate_ref.1, f32[16,256,256]{2,1,0:T(8,128)} %bitcast.12, f32[2,4,256,256]{3,2,1,0:T(8,128)} %copy-done.1, ...), custom_call_target="tpu_custom_call" | custom-call | flops 314572800 | bytes 12582912 | tf_op jit(solution)/shard_map/fields/pallas_call | solution.py:438
  100.2 28.1 %filtered.1 = f32[8,32,128]{2,1,0:T(8,128)} custom-call(f32[8,128,128]{2,1,0:T(8,128)} %fields.1.coarse, f32[4,64,128]{2,1,0:T(8,128)} %divide_multiply_fusion.weights, f32[128,128]{1,0:T(8,128)} %sine_add_fusion.x_table.y_table, f32[128,128]{1,0:T(8,128)} %sine_add_fusion.x_table.y_table, f32[64,64]{1,0:T(8,128)} %sine_add_fusion.1.z_table), custom_call_target="tpu_custom_call" | custom-call | flops 393216000 | bytes 1048576 | tf_op jit(solution)/shard_map/filtered/pallas_call | solution.py:611
  128.3 1.6 %copy.13 = f32[8,32,128]{2,1,0:T(8,128)} copy(f32[8,32,128]{2,1,0:T(8,128)} %filtered.1) | data formatting | bytes 262144
  (3 shorter events, 0.1 us)
Async XLA Ops:
  0.0 2.8 %copy-start = (f32[16,256,256]{2,1,0:T(8,128)S(1)}, f32[16,256,256]{2,1,0:T(8,128)}, u32[]{:S(2)}) copy-start(f32[16,256,256]{2,1,0:T(8,128)} %rate_ref.1) | copy-start | bytes 12582916
  4.5 50.8 %collective-permute-start = (f32[2,4,256,256]{3,2,1,0:T(8,128)}, f32[2,4,256,256]{3,2,1,0:T(8,128)S(1)}, u32[]{:S(2)}, u32[]{:S(2)}) collective-permute-start(f32[2,4,256,256]{3,2,1,0:T(8,128)} %pad_maximum_fusion), channel_id=1, source_target_pairs={{0,1},{1,2},{2,3},{3,4},{4,5},{5,6},{6,7},{7,0},{8,9},{9,10},{10,1... | collective-permute-start | bytes 6291464 | tf_op jit(solution)/shard_map/ppermute | solution.py:646
  6.4 48.8 %collective-permute-start.1 = (f32[2,4,256,256]{3,2,1,0:T(8,128)}, f32[2,4,256,256]{3,2,1,0:T(8,128)}, u32[]{:S(2)}, u32[]{:S(2)}) collective-permute-start(f32[2,4,256,256]{3,2,1,0:T(8,128)} %pad_maximum_fusion.1), channel_id=1, source_target_pairs={{1,0},{2,1},{3,2},{4,3},{5,4},{6,5},{7,6},{0,7},{9,8},{10,9},{11,1... | collective-permute-start | bytes 6291464 | tf_op jit(solution)/shard_map/ppermute | solution.py:646
  55.2 1.4 %copy-start.1 = (f32[2,4,256,256]{3,2,1,0:T(8,128)}, f32[2,4,256,256]{3,2,1,0:T(8,128)S(1)}, u32[]{:S(2)}) copy-start(f32[2,4,256,256]{3,2,1,0:T(8,128)S(1)} %collective-permute-done.below) | copy-start | bytes 6291460
